TPU v7x, 512 devices: a whole 4x4x16 slice. The times are simulated.
512 devices in a mesh: site: 32 (over z, core), mode: 16 (over y, x).
Axes of the slice: x: 4, y: 4, z: 16, core: 2. Of those that a mesh axis runs over, the one named last changes fastest.
Arguments:
- vectors: bfloat16 [2, 512, 147456], P(None, 'mode', 'site'), may hold values from -6 to 6
- images: bfloat16 [2, 512, 147456], P(None, 'mode', 'site'), may hold values from -0.02734375 to 0.02734375
- ritz: float32 [2, 512, 512], replicated, may hold values from -0.1875 to 0.1875
Outputs:
- rotated: bfloat16 [2, 512, 147456], P(None, 'mode', 'site')
- projected: float32 [2, 512, 512], replicated
All inputs are finite; a program needn't handle non-finite values.
Results may differ from a plain program's by a relative error of at most 0.0049.
Values may be sent and summed in bfloat16 or wider, within the bound.
No kernel may reach another device: no remote copies, remote signals or barrier semaphores. Data moves between devices by JAX's collectives and lax.ppermute only.
A program may use at most 64 MiB of HBM per device.

v0:
```python
import jax
import jax.numpy as jnp
from jax import lax
from jax.sharding import PartitionSpec as P


def stacked_ritz(coeffs):
    upper = jnp.concatenate([coeffs[0], coeffs[1]], axis=1)
    lower = jnp.concatenate([-coeffs[1], coeffs[0]], axis=1)
    return jnp.concatenate([upper, lower], axis=0)


def gram_blocks(left_rows, right_rows, left_count, right_count):
    products = lax.dot_general(
        left_rows, right_rows, (((1,), (1,)), ((), ())), preferred_element_type=jnp.float32
    )
    real_part = products[:left_count, :right_count] + products[left_count:, right_count:]
    imag_part = products[:left_count, right_count:] - products[left_count:, :right_count]
    return jnp.stack([real_part, imag_part])


def highest_dot(first_matrix, second_matrix):
    return jnp.dot(
        first_matrix,
        second_matrix,
        precision=lax.Precision.HIGHEST,
        preferred_element_type=jnp.float32,
    )


def project(gram, left_coeffs, right_coeffs):
    mixed_re = highest_dot(gram[0], right_coeffs[0]) - highest_dot(gram[1], right_coeffs[1])
    mixed_im = highest_dot(gram[0], right_coeffs[1]) + highest_dot(gram[1], right_coeffs[0])
    result_re = highest_dot(left_coeffs[0].T, mixed_re) + highest_dot(left_coeffs[1].T, mixed_im)
    result_im = highest_dot(left_coeffs[0].T, mixed_im) - highest_dot(left_coeffs[1].T, mixed_re)
    return jnp.stack([result_re, result_im])


def on_device(vectors, images, ritz):
    owned = vectors.shape[1]
    width = vectors.shape[2]
    offset = lax.axis_index("mode") * owned
    ritz_low = ritz.astype(jnp.bfloat16)
    owned_coeffs = lax.dynamic_slice_in_dim(ritz_low, offset, owned, 2)
    own_vectors = vectors.reshape(2 * owned, width)
    empty = jnp.zeros((2 * owned, width), jnp.float32)
    initial = (empty, jnp.zeros((1,), jnp.float32))
    piece = lax.all_gather(vectors, "mode", axis=1, tiled=True)
    amount = piece.shape[1]
    totals = lax.dot_general(
        stacked_ritz(owned_coeffs),
        piece.reshape(2 * amount, width),
        (((0,), (0,)), ((), ())),
        preferred_element_type=jnp.float32,
    )
    totals, gram_part = (totals, initial[1])
    rotated = totals.astype(jnp.bfloat16).reshape(2, owned, width)
    piece = lax.all_gather(images, "mode", axis=1, tiled=True)
    amount = piece.shape[1]
    block = gram_blocks(own_vectors, piece.reshape(2 * amount, width), owned, amount)
    gram_part = block
    left_coeffs = lax.dynamic_slice_in_dim(ritz, offset, owned, 1)
    summed = lax.psum(gram_part, "site")
    projected = lax.psum(project(summed, left_coeffs, ritz), "mode")
    return (rotated, projected)


def solution(mesh):
    placed = (P(None, "mode", "site"), P(None, "mode", "site"), P())
    return jax.shard_map(
        on_device,
        mesh=mesh,
        in_specs=placed,
        out_specs=(P(None, "mode", "site"), P()),
        check_vma=False,
    )
```

profile of v0, /device:TPU:1, one launch (start us, length us, event | category | flops | bytes accessed | tf_op | source)
XLA Modules:
  0.0 534.4 jit_solution(8298503209477267050)
XLA Ops:
  7.2 0.0 all-gather.5.cloned.1.call-start
  7.2 0.7 all-gather.5.cloned.1.call-update
  7.9 0.0 all-reduce.3.cloned.1.call-start
  7.9 99.4 %all-gather.5.cloned.1.call-done = bf16[2,512,4608]{2,1,0:T(8,128)(2,1)} async-done(((bf16[2,32,4608]{2,1,0:T(8,128)(2,1)}), bf16[2,512,4608]{2,1,0:T(8,128)(2,1)}) %all-gather.5.cloned.1.call-update) | async-done | bytes 9437200 | tf_op jit(solution)/shard_map/all_gather | solution.py:58
  107.4 0.0 copy-start
  107.4 6.9 %fusion.29 = f32[64,1024]{1,0:T(8,128)S(1)} fusion(bf16[64,4608]{1,0:T(8,128)(2,1)} %bitcast.53, bf16[1024,4608]{1,0:T(8,128)(2,1)} %bitcast.52), kind=kOutput, calls=%fused_computation.45 | convolution fusion | flops 603979776 | bytes 10289152 | tf_op jit(solution)/shard_map/dot_general | solution.py:14
  114.3 0.7 pad_maximum_fusion.1
  115.0 0.0 all-reduce.3.cloned.1.call-update
  115.0 0.0 all-gather.3.cloned.1.call-start
  115.1 0.7 all-gather.3.cloned.1.call-update
  115.8 0.0 all-reduce.5.cloned.1.call-start
  115.8 195.0 %all-reduce.3.cloned.1.call-done = f32[2,32,512]{2,1,0:T(8,128)} async-done(((f32[2,32,512]{2,1,0:T(8,128)}), f32[2,32,512]{2,1,0:T(8,128)}) %all-reduce.3.cloned.1.call-update) | async-done | bytes 131088 | tf_op jit(solution)/shard_map/psum | solution.py:63
  310.8 0.0 copy-done
  310.8 0.0 copy-start.1
  310.8 1.6 fusion.2
  312.4 1.5 convolution_add_fusion.1
  314.0 1.0 fusion.21
  315.0 0.0 copy-done.1
  315.0 0.7 fusion.6
  315.7 0.7 convolution_subtract_fusion.1
  316.5 1.1 fusion
  317.5 1.0 fusion.22
  318.6 1.1 fusion.1
  319.6 1.5 pad_maximum_fusion
  321.1 0.0 all-reduce.5.cloned.1.call-update
  321.1 0.1 dynamic-slice_convert_fusion
  321.4 79.7 %all-gather.3.cloned.1.call-done = bf16[2,512,4608]{2,1,0:T(8,128)(2,1)} async-done(((bf16[2,32,4608]{2,1,0:T(8,128)(2,1)}), bf16[2,512,4608]{2,1,0:T(8,128)(2,1)}) %all-gather.3.cloned.1.call-update) | async-done | bytes 9437200 | tf_op jit(solution)/shard_map/all_gather | solution.py:48
  401.0 6.4 %convolution_convert_fusion = bf16[64,4608]{1,0:T(8,128)(2,1)} fusion(bf16[1024,4608]{1,0:T(8,128)(2,1)} %bitcast.51, bf16[512,32]{1,0:T(8,128)(2,1)S(1)} %get-tuple-element.5, bf16[512,32]{1,0:T(8,128)(2,1)S(1)} %fusion.28, bf16[512,32]{1,0:T(8,128)(2,1)S(1)} %get-tuple-element.4), kind=kOutput, calls=%fused_computation | convolution fusion | flops 604798976 | bytes 10125312 | tf_op jit(solution)/shard_map/dot_general | solution.py:50
  407.4 117.4 %all-reduce.5.cloned.1.call-done = f32[2,512,512]{2,1,0:T(8,128)} async-done(((f32[2,512,512]{2,1,0:T(8,128)}), f32[2,512,512]{2,1,0:T(8,128)}) %all-reduce.5.cloned.1.call-update) | async-done | bytes 2097168 | tf_op jit(solution)/shard_map/psum | solution.py:64
  524.8 3.1 copy.7
  (3 shorter events, 0.1 us)
Async XLA Ops:
  7.2 100.2 %all-gather.5.cloned.1.call-start = ((), (), s32[]{:S(2)}) async-start(), calls=%async_computation.1 | async-start | bytes 10027008 | tf_op jit(solution)/shard_map/all_gather | solution.py:58
  7.9 302.9 %all-reduce.3.cloned.1.call-start = ((), (), s32[]{:S(2)}) async-start(), calls=%async_computation.2 | async-start | bytes 262144 | tf_op jit(solution)/shard_map/psum | solution.py:63
  107.4 203.4 %copy-start = (f32[2,512,512]{2,1,0:T(8,128)S(1)}, f32[2,512,512]{2,1,0:T(8,128)}, u32[]{:S(2)}) copy-start(f32[2,512,512]{2,1,0:T(8,128)} %param.5) | copy-start | bytes 6291460
  115.0 286.0 %all-gather.3.cloned.1.call-start = ((), (), s32[]{:S(2)}) async-start(), calls=%async_computation | async-start | bytes 10027008 | tf_op jit(solution)/shard_map/all_gather | solution.py:48
  115.8 409.1 %all-reduce.5.cloned.1.call-start = ((), (), s32[]{:S(2)}) async-start(), calls=%async_computation.3 | async-start | bytes 4194304 | tf_op jit(solution)/shard_map/psum | solution.py:64
  310.8 4.2 copy-start.1
Sparse Core Ops, SparseCore 0:
  11.0 96.3 all-gather.4
  115.2 195.5 all-reduce.2
  314.3 86.7 all-gather.2
  405.1 119.6 all-reduce.4
where the time goes:
time: 535 us; the launch traced here: 534 us
  waiting for transfers between devices  493 us (92%)
  matrix products  22.1 us (4%)
  between operations  13.9 us (3%)
    psum x1, waiting for transfers between devices, on_device(): summed = lax.psum(gram_part, 'site')  195 us
    psum x1, waiting for transfers between devices, on_device(): projected = lax.psum(project(summed, left_coeffs, ritz), 'mode')  117 us
    all_gather x1, waiting for transfers between devices, on_device(): piece = lax.all_gather(images, 'mode', axis=1, tiled=True)  99.4 us
    all_gather x1, waiting for transfers between devices, on_device(): piece = lax.all_gather(vectors, 'mode', axis=1, tiled=True)  79.7 us
  transfers between devices with their start and end apart: 4, of which 4 were waited for; matrix products, arithmetic and copies ran while one was open for 3% of the time, Pallas kernels for 0%

commit v1 on v0

v1 whole, which is shorter than its diff:
```python
import functools

import jax
import jax.numpy as jnp
from jax import lax
from jax.experimental import pallas as pl
from jax.experimental.pallas import tpu as pltpu
from jax.sharding import PartitionSpec as P

BF16 = jnp.bfloat16
F32 = jnp.float32
LANES = 128
VMEM_BYTES = 48 * 1024 * 1024

PEERS = 16
OWNED = 32
MODES = PEERS * OWNED
MAIN = 2 * LANES
QUARTER = LANES // 4
TAIL_AT = PEERS * MAIN
ROTATED_ROWS = 144
SHARE_ROWS = 256
PLANES = 4

NT = (((1,), (1,)), ((), ()))


def lane_group(shape):
    return lax.broadcasted_iota(jnp.int32, shape, len(shape) - 1) // QUARTER


def pack_kernel(vectors_ref, images_ref, out_ref):
    sources = (vectors_ref, images_ref)
    for peer in range(PEERS):
        for which, source in enumerate(sources):
            for half in range(2):
                at = peer * MAIN + half * LANES
                for part in range(2):
                    row = ((which * 2 + half) * 2 + part) * OWNED
                    out_ref[peer, row : row + OWNED, :] = source[part, :, at : at + LANES]
    group = lane_group((OWNED, LANES))
    for block in range(PEERS // 4):
        at = TAIL_AT + block * LANES
        tails = [sources[which][part, :, at : at + LANES].astype(F32) for part in range(2) for which in range(2)]
        for quarter in range(4):
            packed = jnp.zeros((OWNED, LANES), F32)
            for slot, tail in enumerate(tails):
                shift = (slot - quarter) % 4 * QUARTER
                moved = pltpu.roll(tail, shift, 1) if shift else tail
                packed = jnp.where(group == slot, moved, packed)
            out_ref[block * 4 + quarter, 8 * OWNED : 9 * OWNED, :] = packed.astype(BF16)


def coefficients_kernel(ritz_ref, high_ref, low_ref):
    real, imag = ritz_ref[0].T, ritz_ref[1].T
    for row, column, block in ((0, 0, real), (0, 1, -imag), (1, 0, imag), (1, 1, real)):
        high = block.astype(BF16)
        rows, columns = pl.ds(row * MODES, MODES), pl.ds(column * MODES, MODES)
        high_ref[rows, columns] = high
        low_ref[rows, columns] = (block - high.astype(F32)).astype(BF16)


def split(values):
    high = values.astype(BF16)
    return high, (values - high.astype(F32)).astype(BF16)


def local_kernel(got_ref, high_ref, low_ref, out_ref, stacked, tail, left, right):
    for part in range(2):
        rows = slice(part * MODES, (part + 1) * MODES)
        for block in range(4):
            at = (block * 2 + part) * OWNED
            stacked[rows, block * LANES : (block + 1) * LANES] = got_ref[:, at : at + OWNED, :].reshape(MODES, LANES)
    packed = got_ref[:, 8 * OWNED : 9 * OWNED, :].reshape(MODES, LANES)
    stacked[0:MODES, 4 * LANES : 5 * LANES] = packed
    stacked[MODES : 2 * MODES, 4 * LANES : 5 * LANES] = pltpu.roll(packed.astype(F32), 2 * QUARTER, 1).astype(BF16)

    tile = 256
    group = lane_group((tile, LANES))
    for step in range(2 * MODES // tile):
        part, at = divmod(step * tile, MODES)
        rows = slice(step * tile, (step + 1) * tile)
        rotated = jnp.dot(high_ref[rows, :], stacked[...], preferred_element_type=F32)
        for block in range(2):
            values = rotated[:, block * LANES : (block + 1) * LANES].astype(BF16).reshape(tile // OWNED, OWNED, LANES)
            row = (block * 2 + part) * OWNED
            out_ref[at // OWNED : (at + tile) // OWNED, row : row + OWNED, :] = values
        tail[rows, :] = rotated[:, 4 * LANES : 5 * LANES]
        exact = rotated + jnp.dot(low_ref[rows, :], stacked[...], preferred_element_type=F32)
        here = slice(at, at + tile)
        for side, target in enumerate((left, right)):
            for index, values in enumerate(split(exact[:, side * MAIN : (side + 1) * MAIN])):
                target[index, here, part * MAIN : (part + 1) * MAIN] = values
            ends = exact[:, 4 * LANES : 5 * LANES]
            shift = (part - side) % 4 * QUARTER
            ends = pltpu.roll(ends, shift, 1) if shift else ends
            if part == 0:
                ends = jnp.where(group == 0, ends, 0.0)
            else:
                ends = jnp.where(group == 1, ends, 0.0)
            for index, values in enumerate(split(ends)):
                columns = slice(2 * MAIN, 2 * MAIN + LANES)
                if part == 0:
                    target[index, here, columns] = values
                else:
                    target[index, here, columns] = target[index, here, columns] + values

    group = lane_group((PEERS, 16, LANES))
    quarters = [tail[part * MODES : (part + 1) * MODES, :].reshape(PEERS, OWNED, LANES)[:, 16 * half : 16 * half + 16, :]
                for part in range(2) for half in range(2)]
    ends = quarters[0]
    for slot in range(1, 4):
        ends = jnp.where(group == slot, pltpu.roll(quarters[slot], slot * QUARTER, 2), ends)
    out_ref[:, 4 * OWNED : 4 * OWNED + 16, :] = ends.astype(BF16)

    for column in range(4):
        here = slice(column * LANES, (column + 1) * LANES)
        group = lane_group((LANES, LANES))
        real, imag = [], []
        for index in range(2):
            re = right[index, here, 0:MAIN]
            im = right[index, here, MAIN : 2 * MAIN]
            ends = right[index, here, 2 * MAIN : 2 * MAIN + LANES].astype(F32)
            swapped = jnp.where(group == 0, pltpu.roll(ends, LANES - QUARTER, 1), -pltpu.roll(ends, QUARTER, 1))
            swapped = jnp.where(group < 2, swapped, 0.0)
            real.append(right[index, here, :])
            imag.append(jnp.concatenate([im, -re, swapped.astype(BF16)], axis=1))
        for part, sides in enumerate((real, imag)):
            share = lax.dot_general(left[0], sides[0], NT, preferred_element_type=F32)
            share += lax.dot_general(left[0], sides[1], NT, preferred_element_type=F32)
            share += lax.dot_general(left[1], sides[0], NT, preferred_element_type=F32)
            row = ROTATED_ROWS + (column * 2 + part) * OWNED
            out_ref[:, row : row + OWNED, :] = share.astype(BF16).reshape(PEERS, OWNED, LANES)


def unpack_kernel(back_ref, out_ref):
    for peer in range(PEERS):
        for half in range(2):
            at = peer * MAIN + half * LANES
            for part in range(2):
                row = (half * 2 + part) * OWNED
                out_ref[part, :, at : at + LANES] = back_ref[peer, row : row + OWNED, :]
    group = lane_group((16, LANES))
    for block in range(PEERS // 4):
        ends = [back_ref[block * 4 + quarter, 4 * OWNED : 4 * OWNED + 16, :].astype(F32) for quarter in range(4)]
        at = TAIL_AT + block * LANES
        for slot in range(4):
            values = jnp.zeros((16, LANES), F32)
            for quarter, end in enumerate(ends):
                shift = (quarter - slot) % 4 * QUARTER
                moved = pltpu.roll(end, shift, 1) if shift else end
                values = jnp.where(group == quarter, moved, values)
            part, half = divmod(slot, 2)
            out_ref[part, 16 * half : 16 * half + 16, at : at + LANES] = values.astype(BF16)


def widen_kernel(pieces_ref, out_ref):
    for peer in range(PEERS):
        for column in range(4):
            for part in range(2):
                row = (column * 2 + part) * OWNED
                out_ref[part, peer * OWNED : (peer + 1) * OWNED, column * LANES : (column + 1) * LANES] = pieces_ref[
                    peer, row : row + OWNED, :
                ].astype(F32)


def call(kernel, name, outs, *args, flops=0, scratch=()):
    outs = tuple(jax.ShapeDtypeStruct(shape, dtype) for shape, dtype in outs)
    moved = sum(a.size * a.dtype.itemsize for a in args + outs)
    return pl.pallas_call(
        kernel,
        name=name,
        out_shape=outs if len(outs) > 1 else outs[0],
        in_specs=[pl.BlockSpec(memory_space=pltpu.VMEM)] * len(args),
        out_specs=(
            [pl.BlockSpec(memory_space=pltpu.VMEM)] * len(outs)
            if len(outs) > 1
            else pl.BlockSpec(memory_space=pltpu.VMEM)
        ),
        scratch_shapes=list(scratch),
        cost_estimate=pl.CostEstimate(flops=flops, bytes_accessed=moved, transcendentals=0),
        compiler_params=pltpu.CompilerParams(vmem_limit_bytes=VMEM_BYTES),
    )(*args)


def exchange(pieces, axis, groups=None):
    return lax.all_to_all(pieces, axis, 0, 0, axis_index_groups=groups)


def spread(piece, count, axis, groups=None):
    return exchange(jnp.broadcast_to(piece[None], (count,) + piece.shape), axis, groups)


def on_device(site_count, vectors, images, ritz):
    near = 2 * PLANES
    far = site_count // near
    near_groups = [[near * h + i for i in range(near)] for h in range(far)]
    far_groups = [[near * h + i for h in range(far)] for i in range(near)]

    high, low = call(
        coefficients_kernel, "coefficients", [((2 * MODES, 2 * MODES), BF16)] * 2, ritz
    )
    packed = call(pack_kernel, "pack", [((PEERS, 9 * OWNED, LANES), BF16)], vectors, images)
    got = exchange(packed, "mode")
    shares = call(
        local_kernel,
        "rotate_and_project",
        [((PEERS, ROTATED_ROWS + SHARE_ROWS, LANES), BF16)],
        got,
        high,
        low,
        flops=5 * 10**9,
        scratch=[
            pltpu.VMEM((2 * MODES, 5 * LANES), BF16),
            pltpu.VMEM((2 * MODES, LANES), F32),
            pltpu.VMEM((2, MODES, 5 * LANES), BF16),
            pltpu.VMEM((2, MODES, 5 * LANES), BF16),
        ],
    )
    back = exchange(shares, "mode")
    rotated = call(unpack_kernel, "unpack", [((2, OWNED, PEERS * MAIN + 4 * LANES), BF16)], back)

    summed = jnp.sum(back[:, ROTATED_ROWS:, :].astype(F32), axis=0)
    summed = jnp.sum(exchange(summed.reshape(near, OWNED, LANES), "site", near_groups), axis=0)
    summed = jnp.sum(spread(summed, far, "site", far_groups), axis=0)
    rows = spread(summed.astype(BF16), near, "site", near_groups)
    pieces = spread(rows.reshape(SHARE_ROWS, LANES), PEERS, "mode")
    projected = call(widen_kernel, "widen", [((2, MODES, MODES), F32)], pieces)
    return rotated, projected


def solution(mesh):
    placed = (P(None, "mode", "site"), P(None, "mode", "site"), P())
    return jax.shard_map(
        functools.partial(on_device, mesh.shape["site"]),
        mesh=mesh,
        in_specs=placed,
        out_specs=(P(None, "mode", "site"), P()),
        check_vma=False,
    )
```

time: 535 us -> 136 us (0.25)
  waiting for transfers between devices: 493 us -> 27.5 us
  blocking collectives: 0 us -> 76.3 us
  matrix products: 22.1 us -> 0 us
  Pallas kernels: 0 us -> 15.4 us
  between operations: 13.9 us -> 0.7 us
  starting transfers between devices: 0.16 us -> 11.2 us
    psum x2 -> x0, waiting for transfers between devices: 312 us -> none  [the longest x1 195 us: on_device(): summed = lax.psum(gram_part, 'site')]
    all_gather x2 -> x0, waiting for transfers between devices: 179 us -> none  [the longest x1 99.4 us: on_device(): piece = lax.all_gather(images, 'mode', axis=1, tiled=True)]
    all_to_all x0 -> x4, blocking collectives: none -> 76.3 us  [exchange(): return lax.all_to_all(pieces, axis, 0, 0, axis_index_groups=groups)]
    all_to_all x0 -> x2, waiting for transfers between devices: none -> 27.5 us  [exchange(): return lax.all_to_all(pieces, axis, 0, 0, axis_index_groups=groups)]
    dot_general x10 -> x0, matrix products: 22.1 us -> none  [the longest x8 8.76 us: highest_dot(): jnp.dot(first_matrix, second_matrix, precision=lax.Precision.HIGHEST, pre...]
    pallas_call x0 -> x5, Pallas kernels: none -> 15.4 us  [call(): pl.pallas_call(kernel, name=name, out_shape=outs if len(outs) > 1 else ou...]
    all_to_all x0 -> x2, starting transfers between devices: none -> 11.2 us  [exchange(): return lax.all_to_all(pieces, axis, 0, 0, axis_index_groups=groups)]
  transfers between devices with their start and end apart: 4 -> 2, of which waited for: 4 -> 2; matrix products, arithmetic and copies ran while one was open for 3% -> 0% of each run, Pallas kernels for 0% -> 2%
where the time goes in v1:
time: 136 us
  blocking collectives  76.3 us (56%)
  waiting for transfers between devices  27.5 us (20%)
  Pallas kernels  15.4 us (11%)
  starting transfers between devices  11.2 us (8%)
  local copies, waits for them, and re-layouts  4.63 us (3%)
    all_to_all x4, blocking collectives, exchange(): return lax.all_to_all(pieces, axis, 0, 0, axis_index_groups=groups)  76.3 us
    all_to_all x2, waiting for transfers between devices, exchange(): return lax.all_to_all(pieces, axis, 0, 0, axis_index_groups=groups)  27.5 us
    pallas_call x5, Pallas kernels, call(): pl.pallas_call(kernel, name=name, out_shape=outs if len(outs) > 1 else ou...  15.4 us
    all_to_all x2, starting transfers between devices, exchange(): return lax.all_to_all(pieces, axis, 0, 0, axis_index_groups=groups)  11.2 us
    unnamed x6, local copies, waits for them, and re-layouts  3.43 us
  transfers between devices with their start and end apart: 2, of which 2 were waited for; matrix products, arithmetic and copies ran while one was open for 0% of the time, Pallas kernels for 2%

profile of v1, /device:TPU:1, one launch (start us, length us, event | category | flops | bytes accessed | tf_op | source)
XLA Modules:
  0.0 135.9 jit_solution(6316179093093333442)
XLA Ops:
  0.6 0.0 copy-start
  0.6 1.1 copy-done
  1.7 0.0 copy-start.1
  1.7 1.1 copy-done.1
  2.8 1.3 pack.1
  4.1 7.6 %all-to-all-start = ((bf16[16,288,128]{2,1,0:T(8,128)(2,1)}), bf16[16,288,128]{2,1,0:T(8,128)(2,1)S(1)}, u32[]{:S(2)}, u32[]{:S(2)}) async-start(bf16[16,288,128]{2,1,0:T(8,128)(2,1)} %pack.1), calls=%async_computation | async-start | bytes 2359296 | tf_op jit(solution)/shard_map/all_to_all | solution.py:187
  11.6 2.3 %coefficients.1 = (bf16[1024,1024]{1,0:T(8,128)(2,1)S(1)}, bf16[1024,1024]{1,0:T(8,128)(2,1)S(1)}) custom-call(f32[2,512,512]{2,1,0:T(8,128)} %ritz_ref.1), custom_call_target="tpu_custom_call" | custom-call | bytes 6291456 | tf_op jit(solution)/shard_map/coefficients/pallas_call | solution.py:170
  13.9 0.0 copy-start.2
  13.9 1.3 copy-done.2
  15.2 12.4 %all-to-all-done.got_ref = bf16[16,288,128]{2,1,0:T(8,128)(2,1)S(1)} async-done(((bf16[16,288,128]{2,1,0:T(8,128)(2,1)}), bf16[16,288,128]{2,1,0:T(8,128)(2,1)S(1)}, u32[]{:S(2)}, u32[]{:S(2)}) %all-to-all-start) | async-done | bytes 1179680 | tf_op jit(solution)/shard_map/all_to_all | solution.py:187
  27.6 9.4 %rotate_and_project.1 = bf16[16,400,128]{2,1,0:T(8,128)(2,1)S(1)} custom-call(bf16[16,288,128]{2,1,0:T(8,128)(2,1)S(1)} %all-to-all-done.got_ref, bf16[1024,1024]{1,0:T(8,128)(2,1)S(1)} %get-tuple-element.4.high_ref, bf16[1024,1024]{1,0:T(8,128)(2,1)} %copy-done.2), custom_call_target="tpu_custom_call" | custom-call | flops 5000000000 | bytes 7012352 | tf_op jit(solution)/shard_map/rotate_and_project/pallas_call | solution.py:170
  37.0 24.5 %all_to_all.30.back_ref = bf16[16,400,128]{2,1,0:T(8,128)(2,1)S(1)} all-to-all(bf16[16,400,128]{2,1,0:T(8,128)(2,1)S(1)} %rotate_and_project.1), channel_id=1, replica_groups=mesh['site'=32,'mode'=16] {'mode'}, dimensions={0} | all-to-all | bytes 3276800 | tf_op jit(solution)/shard_map/all_to_all | solution.py:187
  61.5 0.1 convert_reduce_fusion
  61.7 17.7 %all_to_all.31 = f32[8,32,128]{2,1,0:T(8,128)S(1)} all-to-all(f32[8,32,128]{2,1,0:T(8,128)S(1)} %bitcast.2), channel_id=1, replica_groups={{0,16,32,48,64,80,96,112},{128,144,160,176,192,208,224,240},{256,272,28..., dimensions={0} | all-to-all | bytes 262144 | tf_op jit(solution)/shard_map/all_to_all | solution.py:187
  79.4 24.3 %all_to_all.32 = f32[4,32,128]{2,1,0:T(8,128)S(1)} all-to-all(f32[4,32,128]{2,1,0:T(8,128)S(1)} %broadcast_in_dim.8), channel_id=1, replica_groups={{0,128,256,384},{16,144,272,400},{32,160,288,416},{48,176,304,432},{64,..., dimensions={0} | all-to-all | bytes 131072 | tf_op jit(solution)/shard_map/all_to_all | solution.py:187
  103.7 9.9 %all_to_all.33 = bf16[8,32,128]{2,1,0:T(8,128)(2,1)S(1)} all-to-all(bf16[8,32,128]{2,1,0:T(8,128)(2,1)S(1)} %broadcast_in_dim.9), channel_id=1, replica_groups={{0,16,32,48,64,80,96,112},{128,144,160,176,192,208,224,240},{256,272,28..., dimensions={0} | all-to-all | bytes 131072 | tf_op jit(solution)/shard_map/all_to_all | solution.py:187
  113.5 1.2 broadcast_in_dim.22
  114.7 3.7 %all-to-all-start.5 = ((bf16[16,256,128]{2,1,0:T(8,128)(2,1)}), bf16[16,256,128]{2,1,0:T(8,128)(2,1)S(1)}, u32[]{:S(2)}, u32[]{:S(2)}) async-start(bf16[16,256,128]{2,1,0:T(8,128)(2,1)} %broadcast_in_dim.22), calls=%async_computation.5 | async-start | bytes 2097152 | tf_op jit(solution)/shard_map/all_to_all | solution.py:187
  118.4 1.0 unpack.1
  119.3 15.1 %all-to-all-done.5.pieces_ref = bf16[16,256,128]{2,1,0:T(8,128)(2,1)S(1)} async-done(((bf16[16,256,128]{2,1,0:T(8,128)(2,1)}), bf16[16,256,128]{2,1,0:T(8,128)(2,1)S(1)}, u32[]{:S(2)}, u32[]{:S(2)}) %all-to-all-start.5) | async-done | bytes 1048608 | tf_op jit(solution)/shard_map/all_to_all | solution.py:187
  134.4 1.5 %widen.1 = f32[2,512,512]{2,1,0:T(8,128)} custom-call(bf16[16,256,128]{2,1,0:T(8,128)(2,1)S(1)} %all-to-all-done.5.pieces_ref), custom_call_target="tpu_custom_call" | custom-call | bytes 3145728 | tf_op jit(solution)/shard_map/widen/pallas_call | solution.py:170
  (4 shorter events, 0.0 us)
Async XLA Ops:
  0.6 1.1 copy-start
  1.7 1.1 copy-start.1
  4.1 23.6 %all-to-all-start = ((bf16[16,288,128]{2,1,0:T(8,128)(2,1)}), bf16[16,288,128]{2,1,0:T(8,128)(2,1)S(1)}, u32[]{:S(2)}, u32[]{:S(2)}) async-start(bf16[16,288,128]{2,1,0:T(8,128)(2,1)} %pack.1), calls=%async_computation | async-start | bytes 2359296 | tf_op jit(solution)/shard_map/all_to_all | solution.py:187
  13.9 1.3 copy-start.2
  114.7 19.7 %all-to-all-start.5 = ((bf16[16,256,128]{2,1,0:T(8,128)(2,1)}), bf16[16,256,128]{2,1,0:T(8,128)(2,1)S(1)}, u32[]{:S(2)}, u32[]{:S(2)}) async-start(bf16[16,256,128]{2,1,0:T(8,128)(2,1)} %broadcast_in_dim.22), calls=%async_computation.5 | async-start | bytes 2097152 | tf_op jit(solution)/shard_map/all_to_all | solution.py:187

commit v2 on v0

v2 whole, which is shorter than its diff:
```python
import functools

import jax
import jax.numpy as jnp
from jax import lax
from jax.experimental import pallas as pl
from jax.experimental.pallas import tpu as pltpu
from jax.sharding import PartitionSpec as P

BF16 = jnp.bfloat16
F32 = jnp.float32
LANES = 128
MIB = 1024 * 1024

PEERS = 16
OWNED = 32
HALF = OWNED // 2
MODES = PEERS * OWNED
HALF_MODES = MODES // 2
MAIN = 2 * LANES
QUARTER = LANES // 4
TAIL_AT = PEERS * MAIN
TAIL_ROW = 4 * OWNED
PIECE_ROWS = TAIL_ROW + HALF
DEPTH = 2 * MAIN + LANES
SHARE_ROWS = 8 * HALF
CHUNKS = 4
NEAR = 4
ROWS = HALF // NEAR

NT = (((1,), (1,)), ((), ()))


def lane_group(shape):
    return lax.broadcasted_iota(jnp.int32, shape, len(shape) - 1) // QUARTER


def turn(values, groups):
    shift = groups % 4 * QUARTER
    return pltpu.roll(values, shift, len(values.shape) - 1) if shift else values


def pack_kernel(vectors_hbm, images_hbm, out_hbm, vectors_ref, images_ref, out_ref, arrived, sent):
    peers = PEERS // CHUNKS
    copies = []
    for which, (source, target) in enumerate(((vectors_hbm, vectors_ref), (images_hbm, images_ref))):
        for chunk in range(CHUNKS + 1):
            at = chunk * peers * MAIN
            lanes = pl.ds(at, TAIL_AT // CHUNKS if chunk < CHUNKS else 4 * LANES)
            copy = pltpu.make_async_copy(
                source.at[:, :, lanes], target.at[:, :, lanes], arrived.at[which * (CHUNKS + 1) + chunk]
            )
            copy.start()
            copies.append(copy)
    group = lane_group((HALF, LANES))
    leaving = []
    for which, source_ref in enumerate((vectors_ref, images_ref)):
        base = which * PIECE_ROWS
        for chunk in range(CHUNKS + 1):
            index = which * (CHUNKS + 1) + chunk
            copies[index].wait()
            if chunk < CHUNKS:
                for peer in range(chunk * peers, (chunk + 1) * peers):
                    for block in range(2):
                        at = peer * MAIN + block * LANES
                        for part in range(2):
                            row = base + (block * 2 + part) * OWNED
                            out_ref[peer, row : row + OWNED, :] = source_ref[part, :, at : at + LANES]
                where = (pl.ds(chunk * peers, peers), pl.ds(base, TAIL_ROW))
            else:
                for block in range(PEERS // 4):
                    at = TAIL_AT + block * LANES
                    tails = [
                        source_ref[part, half * HALF : (half + 1) * HALF, at : at + LANES].astype(F32)
                        for part in range(2)
                        for half in range(2)
                    ]
                    for quarter in range(4):
                        packed = turn(tails[0], -quarter)
                        for slot in range(1, 4):
                            packed = jnp.where(group == slot, turn(tails[slot], slot - quarter), packed)
                        out_ref[block * 4 + quarter, base + TAIL_ROW : base + PIECE_ROWS, :] = packed.astype(BF16)
                where = (pl.ds(0, PEERS), pl.ds(base + TAIL_ROW, HALF))
            copy = pltpu.make_async_copy(out_ref.at[where], out_hbm.at[where], sent.at[index])
            copy.start()
            leaving.append(copy)
    for copy in leaving:
        copy.wait()


def unpack_kernel(back_ref, out_ref):
    for peer in range(PEERS):
        for block in range(2):
            at = peer * MAIN + block * LANES
            for part in range(2):
                row = SHARE_ROWS + (block * 2 + part) * OWNED
                out_ref[part, :, at : at + LANES] = back_ref[peer, row : row + OWNED, :]
    group = lane_group((HALF, LANES))
    for block in range(PEERS // 4):
        ends = [back_ref[block * 4 + quarter, SHARE_ROWS + TAIL_ROW : SHARE_ROWS + PIECE_ROWS, :].astype(F32) for quarter in range(4)]
        at = TAIL_AT + block * LANES
        for slot in range(4):
            values = turn(ends[0], -slot)
            for quarter in range(1, 4):
                values = jnp.where(group == quarter, turn(ends[quarter], quarter - slot), values)
            part, half = divmod(slot, 2)
            out_ref[part, half * HALF : (half + 1) * HALF, at : at + LANES] = values.astype(BF16)


def split(values):
    high = values.astype(BF16)
    return high, (values - high.astype(F32)).astype(BF16)


def turn_kernel(ritz_ref, turn_ref):
    real, imag = ritz_ref[0].T, ritz_ref[1].T
    for row, column, block in ((0, 0, real), (0, 1, -imag), (1, 0, imag), (1, 1, real)):
        turn_ref[row * MODES : (row + 1) * MODES, column * MODES : (column + 1) * MODES] = block.astype(BF16)


def split_kernel(ritz_ref, high_ref, low_ref):
    for part in range(2):
        high_ref[part], low_ref[part] = split(ritz_ref[part])


def left_kernel(ritz_ref, left_high_ref, left_low_ref):
    groups = (PEERS, 2, HALF // 8, 8, MODES)
    first = lax.broadcasted_iota(jnp.int32, (PEERS, 8, MODES), 1) < ROWS
    real, imag = ritz_ref[0].reshape(groups), ritz_ref[1].reshape(groups)
    for core in range(2):
        for part in range(2):
            blocks = []
            for pair in range(HALF // 8):
                one, two = (real, imag) if part == 0 else (-imag, real)
                one, two = one[:, core, pair], two[:, core, pair]
                blocks.append(jnp.where(first, one, pltpu.roll(two, ROWS, 1)))
                blocks.append(jnp.where(first, pltpu.roll(one, ROWS, 1), two))
            values = jnp.concatenate(blocks, axis=1).reshape(MODES, MODES).T
            rows = slice(part * MODES, (part + 1) * MODES)
            left_high_ref[core, rows, :], left_low_ref[core, rows, :] = split(values)


def rotate_kernel(got_ref, turn_ref, out_ref, stacked):
    packed = got_ref[:, TAIL_ROW:PIECE_ROWS, :].astype(F32)
    for part in range(2):
        rows = slice(part * MODES, (part + 1) * MODES)
        for block in range(2):
            at = (block * 2 + part) * OWNED
            stacked[rows, block * LANES : (block + 1) * LANES] = got_ref[:, at : at + OWNED, :].reshape(MODES, LANES)
        ends = jnp.concatenate([turn(packed, -2 * part), turn(packed, -2 * part - 1)], axis=1)
        stacked[rows, MAIN : MAIN + LANES] = ends.reshape(MODES, LANES).astype(BF16)

    owners = HALF_MODES // OWNED
    group = lane_group((owners, HALF, LANES))
    for step in range(2):
        peers = slice(step * owners, (step + 1) * owners)
        sent = None
        for part in range(2):
            at = part * MODES + step * HALF_MODES
            rotated = jnp.dot(turn_ref[at : at + HALF_MODES, :], stacked[...], preferred_element_type=F32)
            for block in range(2):
                row = (block * 2 + part) * OWNED
                values = rotated[:, block * LANES : (block + 1) * LANES].astype(BF16)
                out_ref[peers, row : row + OWNED, :] = values.reshape(owners, OWNED, LANES)
            ends = rotated[:, MAIN : MAIN + LANES].reshape(owners, OWNED, LANES)
            for half in range(2):
                moved = turn(ends[:, half * HALF : (half + 1) * HALF, :], part * 2 + half)
                sent = moved if sent is None else jnp.where(group == part * 2 + half, moved, sent)
        out_ref[peers, TAIL_ROW:PIECE_ROWS, :] = sent.astype(BF16)


def share_kernel(other, got_ref, out_ref, left, right):
    core = lax.rem(lax.axis_index("site"), 2)
    half = 1 - core if other else core
    group = lane_group((PEERS, HALF, LANES))

    def side(packed, row_half, sources, signs):
        first, second = (turn(packed, place - 2 * sources[place] - row_half) * signs[place] for place in range(2))
        return jnp.where(group == 0, first, jnp.where(group == 1, second, 0.0))

    packed = got_ref[:, TAIL_ROW:PIECE_ROWS, :].astype(F32)
    for part in range(2):
        for block in range(2):
            row = pl.multiple_of((block * 2 + part) * OWNED + half * HALF, HALF)
            at = part * MAIN + block * LANES
            left[:, at : at + LANES] = got_ref[:, pl.ds(row, HALF), :].reshape(HALF_MODES, LANES)
    ends = jnp.where(half == 0, side(packed, 0, (0, 1), (1, 1)), side(packed, 1, (0, 1), (1, 1)))
    left[:, 2 * MAIN : DEPTH] = ends.reshape(HALF_MODES, LANES).astype(BF16)

    packed = got_ref[:, PIECE_ROWS + TAIL_ROW : 2 * PIECE_ROWS, :].astype(F32)
    for part in range(2):
        sources, signs = ((0, 1), (1, 1)) if part == 0 else ((1, 0), (1, -1))
        for place in range(2):
            for block in range(2):
                at = PIECE_ROWS + (block * 2 + sources[place]) * OWNED
                values = got_ref[:, at : at + OWNED, :].reshape(MODES, LANES)
                lanes = slice(place * MAIN + block * LANES, place * MAIN + (block + 1) * LANES)
                right[part, :, lanes] = values if signs[place] > 0 else -values
        ends = jnp.concatenate([side(packed, row_half, sources, signs) for row_half in range(2)], axis=1)
        right[part, :, 2 * MAIN : DEPTH] = ends.reshape(MODES, LANES).astype(BF16)
    for part in range(2):
        share = lax.dot_general(left[...], right[part], NT, preferred_element_type=F32)
        for column in range(4):
            row = (part * 4 + column) * HALF
            values = share[:, column * LANES : (column + 1) * LANES].reshape(PEERS, HALF, LANES)
            out_ref[:, row : row + HALF, :] = values.astype(out_ref.dtype)


def assemble_kernel(kept_ref, taken_ref, turned_ref, out_ref):
    out_ref[:, 0:SHARE_ROWS, :] = (kept_ref[...] + taken_ref[...].astype(F32)).astype(BF16)
    out_ref[:, SHARE_ROWS:, :] = turned_ref[...]


def sum_kernel(back_ref, out_ref):
    total = back_ref[0, 0:SHARE_ROWS, :].astype(F32)
    for peer in range(1, PEERS):
        total += back_ref[peer, 0:SHARE_ROWS, :].astype(F32)
    for part in range(2):
        for column in range(4):
            at = (part * 4 + column) * HALF
            for near in range(NEAR):
                out_ref[near, part * ROWS : (part + 1) * ROWS, column * LANES : (column + 1) * LANES] = total[
                    at + near * ROWS : at + (near + 1) * ROWS, :
                ]


def project_kernel(far_ref, high_ref, low_ref, out_ref):
    total = far_ref[0]
    for peer in range(1, far_ref.shape[0]):
        total += far_ref[peer]
    high, low = split(total)
    both = jnp.concatenate([high.astype(F32), low.astype(F32)], axis=0).astype(BF16)
    products = []
    for part in range(2):
        first = jnp.dot(both, high_ref[part], preferred_element_type=F32)
        second = jnp.dot(both, low_ref[part], preferred_element_type=F32)
        products.append(first[0 : 2 * ROWS] + first[2 * ROWS : 4 * ROWS] + second[0 : 2 * ROWS])
    real = products[0][0:ROWS] - products[1][ROWS : 2 * ROWS]
    imag = products[0][ROWS : 2 * ROWS] + products[1][0:ROWS]
    rows = jnp.concatenate([real, imag], axis=0)
    for near in range(NEAR):
        out_ref[near] = rows


def finish_products(half, rows_ref, high_ref, low_ref, here):
    rows = rows_ref[...].reshape(MODES, MODES)
    total = jnp.dot(high_ref[half, here, :], rows, preferred_element_type=F32)
    return total + jnp.dot(low_ref[half, here, :], rows, preferred_element_type=F32)


def finish_own_kernel(rows_ref, high_ref, low_ref, out_ref):
    core = lax.rem(lax.axis_index("site"), 2)
    for part in range(2):
        out_ref[part] = finish_products(core, rows_ref, high_ref, low_ref, pl.ds(part * MODES, MODES))


def finish_other_kernel(rows_ref, high_ref, low_ref, first_ref, out_hbm, total, sent):
    core = lax.rem(lax.axis_index("site"), 2)
    copies = []
    for part in range(2):
        for half in range(2):
            rows = pl.ds(half * HALF_MODES, HALF_MODES)
            here = pl.ds(part * MODES + half * HALF_MODES, HALF_MODES)
            total[part, rows, :] = first_ref[part, rows, :] + finish_products(1 - core, rows_ref, high_ref, low_ref, here)
            copy = pltpu.make_async_copy(total.at[part, rows, :], out_hbm.at[part, rows, :], sent.at[part * 2 + half])
            copy.start()
            copies.append(copy)
    for copy in copies:
        copy.wait()


def call(kernel, name, outs, *args, flops=0, scratch=(), in_place=False, out_place=False, vmem=16):
    outs = tuple(jax.ShapeDtypeStruct(shape, dtype) for shape, dtype in outs)
    moved = sum(a.size * a.dtype.itemsize for a in args + outs)
    whole = pl.BlockSpec(memory_space=pltpu.VMEM)
    source = pl.BlockSpec(memory_space=pltpu.HBM) if in_place else whole
    target = pl.BlockSpec(memory_space=pltpu.HBM) if out_place else whole
    single = len(outs) == 1
    return pl.pallas_call(
        kernel,
        name=name,
        out_shape=outs[0] if single else outs,
        in_specs=[source] * len(args),
        out_specs=target if single else [target] * len(outs),
        scratch_shapes=list(scratch),
        cost_estimate=pl.CostEstimate(flops=flops, bytes_accessed=moved, transcendentals=0),
        compiler_params=pltpu.CompilerParams(vmem_limit_bytes=vmem * MIB),
    )(*args)


def exchange(pieces, axis, groups=None):
    return lax.all_to_all(pieces, axis, 0, 0, axis_index_groups=groups)


def spread(piece, count):
    return jnp.broadcast_to(piece[None], (count,) + piece.shape)


def on_device(site_count, vectors, images, ritz):
    far = site_count // (2 * NEAR)
    near_groups = [[2 * (NEAR * h + z) + c for z in range(NEAR)] for h in range(far) for c in range(2)]
    far_groups = [[2 * (NEAR * h + z) + c for h in range(far)] for z in range(NEAR) for c in range(2)]
    swap = [(i, i ^ 1) for i in range(site_count)]
    width = PEERS * MAIN + 4 * LANES
    share = (PEERS, SHARE_ROWS, LANES)
    square = (2 * MODES, 2 * MODES)
    local = [((2, OWNED, width), BF16)]

    packed = call(
        pack_kernel,
        "pack",
        [((PEERS, 2 * PIECE_ROWS, LANES), BF16)],
        vectors,
        images,
        scratch=[
            pltpu.VMEM((2, OWNED, width), BF16),
            pltpu.VMEM((2, OWNED, width), BF16),
            pltpu.VMEM((PEERS, 2 * PIECE_ROWS, LANES), BF16),
            pltpu.SemaphoreType.DMA((2 * CHUNKS + 2,)),
            pltpu.SemaphoreType.DMA((2 * CHUNKS + 2,)),
        ],
        in_place=True,
        out_place=True,
        vmem=60,
    )
    packed, ritz = lax.optimization_barrier((packed, ritz))
    factors = (
        call(turn_kernel, "turn_matrix", [(square, BF16)], ritz),
        call(left_kernel, "left_factors", [((2, 2 * MODES, MODES), BF16)] * 2, ritz),
        call(split_kernel, "split_ritz", [(ritz.shape, BF16)] * 2, ritz),
    )
    got, (turn_matrix, left, ritz_split) = lax.optimization_barrier((exchange(packed, "mode"), factors))

    sides = [pltpu.VMEM((HALF_MODES, DEPTH), BF16), pltpu.VMEM((2, MODES, DEPTH), BF16)]
    given = call(functools.partial(share_kernel, True), "share_given", [(share, BF16)], got, flops=10**9, scratch=sides)
    taken = lax.ppermute(given, "site", swap)
    kept = call(functools.partial(share_kernel, False), "share_kept", [(share, F32)], got, flops=10**9, scratch=sides)
    turned = call(
        rotate_kernel,
        "rotate",
        [((PEERS, PIECE_ROWS, LANES), BF16)],
        got,
        turn_matrix,
        flops=10**9,
        scratch=[pltpu.VMEM((2 * MODES, MAIN + LANES), BF16)],
    )
    sent = call(assemble_kernel, "assemble", [((PEERS, SHARE_ROWS + PIECE_ROWS, LANES), BF16)], kept, taken, turned)
    back = exchange(sent, "mode")
    summed = call(sum_kernel, "sum_shares", [((NEAR, 2 * ROWS, MODES), F32)], back)
    summed = exchange(summed, "site", near_groups)
    summed = exchange(spread(jnp.sum(summed, axis=0), far), "site", far_groups)
    rows = call(project_kernel, "project", [((NEAR, 2 * ROWS, MODES), F32)], summed, *ritz_split)
    rows = exchange(rows, "site", near_groups).reshape(OWNED, MODES).astype(BF16)
    own = exchange(spread(rows, PEERS), "mode")
    own, back = lax.optimization_barrier((own, back))
    other = lax.ppermute(own, "site", swap)
    rotated = call(unpack_kernel, "unpack", local, back)
    whole = [((2, MODES, MODES), F32)]
    first = call(finish_own_kernel, "finish_own", whole, own, *left, flops=10**9)
    projected = call(
        finish_other_kernel,
        "finish_other",
        whole,
        other,
        *left,
        first,
        flops=10**9,
        scratch=[pltpu.VMEM((2, MODES, MODES), F32), pltpu.SemaphoreType.DMA((4,))],
        out_place=True,
    )
    return rotated, projected


def solution(mesh):
    placed = (P(None, "mode", "site"), P(None, "mode", "site"), P())
    return jax.shard_map(
        functools.partial(on_device, mesh.shape["site"]),
        mesh=mesh,
        in_specs=placed,
        out_specs=(P(None, "mode", "site"), P()),
        check_vma=False,
    )
```

time: 535 us -> 123 us (0.23)
  waiting for transfers between devices: 493 us -> 8.06 us
  blocking collectives: 0 us -> 73.2 us
  starting transfers between devices: 0.16 us -> 22.5 us
  matrix products: 22.1 us -> 0 us
  between operations: 13.9 us -> 0.84 us
  Pallas kernels: 0 us -> 12 us
    psum x2 -> x0, waiting for transfers between devices: 312 us -> none  [the longest x1 195 us: on_device(): summed = lax.psum(gram_part, 'site')]
    all_gather x2 -> x0, waiting for transfers between devices: 179 us -> none  [the longest x1 99.4 us: on_device(): piece = lax.all_gather(images, 'mode', axis=1, tiled=True)]
    all_to_all x0 -> x5, blocking collectives: none -> 73.2 us  [exchange(): return lax.all_to_all(pieces, axis, 0, 0, axis_index_groups=groups)]
    dot_general x10 -> x0, matrix products: 22.1 us -> none  [the longest x8 8.76 us: highest_dot(): jnp.dot(first_matrix, second_matrix, precision=lax.Precision.HIGHEST, pre...]
    ppermute x0 -> x2, starting transfers between devices: none -> 14.9 us  [the longest x1 8.77 us: on_device(): other = lax.ppermute(own, 'site', swap)]
    pallas_call x0 -> x13, Pallas kernels: none -> 12 us  [call(): pl.pallas_call(kernel, name=name, out_shape=outs[0] if single else outs,...]
    all_to_all x0 -> x1, waiting for transfers between devices: none -> 8.05 us  [exchange(): return lax.all_to_all(pieces, axis, 0, 0, axis_index_groups=groups)]
    all_to_all x0 -> x1, starting transfers between devices: none -> 7.6 us  [exchange(): return lax.all_to_all(pieces, axis, 0, 0, axis_index_groups=groups)]
  transfers between devices with their start and end apart: 4 -> 3, of which waited for: 4 -> 1; matrix products, arithmetic and copies ran while one was open for 3% -> 0% of each run, Pallas kernels for 0% -> 5%
where the time goes in v2:
time: 123 us
  blocking collectives  73.2 us (60%)
  starting transfers between devices  22.5 us (18%)
  Pallas kernels  12 us (10%)
  waiting for transfers between devices  8.06 us (7%)
  local copies, waits for them, and re-layouts  6 us (5%)
    all_to_all x5, blocking collectives, exchange(): return lax.all_to_all(pieces, axis, 0, 0, axis_index_groups=groups)  73.2 us
    pallas_call x13, Pallas kernels, call(): pl.pallas_call(kernel, name=name, out_shape=outs[0] if single else outs,...  12 us
    ppermute x1, starting transfers between devices, on_device(): other = lax.ppermute(own, 'site', swap)  8.77 us
    all_to_all x1, waiting for transfers between devices, exchange(): return lax.all_to_all(pieces, axis, 0, 0, axis_index_groups=groups)  8.05 us
    all_to_all x1, starting transfers between devices, exchange(): return lax.all_to_all(pieces, axis, 0, 0, axis_index_groups=groups)  7.6 us
    ppermute x1, starting transfers between devices, on_device(): taken = lax.ppermute(given, 'site', swap)  6.15 us
    unnamed x22, local copies, waits for them, and re-layouts  5.96 us
  transfers between devices with their start and end apart: 3, of which 1 were waited for; matrix products, arithmetic and copies ran while one was open for 0% of the time, Pallas kernels for 5%

profile of v2, /device:TPU:1, one launch (start us, length us, event | category | flops | bytes accessed | tf_op | source)
XLA Modules:
  0.0 122.7 jit_solution(7984773489671416835)
XLA Ops:
  0.6 0.0 copy-start
  0.6 2.4 %pack.1 = bf16[16,288,128]{2,1,0:T(8,128)(2,1)} custom-call(bf16[2,32,4608]{2,1,0:T(8,128)(2,1)} %vectors_hbm.1, bf16[2,32,4608]{2,1,0:T(8,128)(2,1)} %images_hbm.1), custom_call_target="tpu_custom_call" | custom-call | bytes 2359296 | tf_op jit(solution)/shard_map/pack/pallas_call | solution.py:279
  3.1 7.6 %all-to-all-start = ((bf16[16,288,128]{2,1,0:T(8,128)(2,1)}), bf16[16,288,128]{2,1,0:T(8,128)(2,1)S(1)}, u32[]{:S(2)}, u32[]{:S(2)}) async-start(bf16[16,288,128]{2,1,0:T(8,128)(2,1)} %pack.1), calls=%async_computation | async-start | bytes 2359296 | tf_op jit(solution)/shard_map/all_to_all | solution.py:292
  10.7 0.0 copy-done
  10.7 0.5 turn_matrix.1.turn_ref
  11.2 0.0 copy-start.5
  11.2 1.3 %copy-done.5 = bf16[1024,1024]{1,0:T(8,128)(2,1)} copy-done((bf16[1024,1024]{1,0:T(8,128)(2,1)}, bf16[1024,1024]{1,0:T(8,128)(2,1)S(1)}, u32[]{:S(2)}) %copy-start.5) | copy-done | bytes 2097176
  12.5 0.3 split_ritz.1
  12.8 0.0 copy-start.7
  12.8 1.0 copy-done.7
  13.8 0.0 copy-start.9
  13.8 1.0 copy-done.9
  14.8 1.2 left_factors.1
  15.9 0.0 copy-start.1
  15.9 1.3 %copy-done.1 = bf16[2,1024,512]{2,1,0:T(8,128)(2,1)} copy-done((bf16[2,1024,512]{2,1,0:T(8,128)(2,1)}, bf16[2,1024,512]{2,1,0:T(8,128)(2,1)S(1)}, u32[]{:S(2)}) %copy-start.1) | copy-done | bytes 2097176
  17.3 0.0 copy-start.3
  17.3 1.3 %copy-done.3 = bf16[2,1024,512]{2,1,0:T(8,128)(2,1)} copy-done((bf16[2,1024,512]{2,1,0:T(8,128)(2,1)}, bf16[2,1024,512]{2,1,0:T(8,128)(2,1)S(1)}, u32[]{:S(2)}) %copy-start.3) | copy-done | bytes 2097176
  18.6 8.1 %all-to-all-done.got_ref = bf16[16,288,128]{2,1,0:T(8,128)(2,1)S(1)} async-done(((bf16[16,288,128]{2,1,0:T(8,128)(2,1)}), bf16[16,288,128]{2,1,0:T(8,128)(2,1)S(1)}, u32[]{:S(2)}, u32[]{:S(2)}) %all-to-all-start) | async-done | bytes 1179680 | tf_op jit(solution)/shard_map/all_to_all | solution.py:292
  26.7 0.7 share_given.1
  27.4 0.0 copy-start.6
  27.4 6.2 %collective-permute-start = (bf16[16,128,128]{2,1,0:T(8,128)(2,1)S(1)}, bf16[16,128,128]{2,1,0:T(8,128)(2,1)S(1)}, u32[]{:S(2)}, u32[]{:S(2)}) collective-permute-start(bf16[16,128,128]{2,1,0:T(8,128)(2,1)S(1)} %share_given.1), channel_id=1, source_target_pairs={{0,16},{16,0},{32,48},{48,32},{64,80},{80,64},{96,112},{112,96},{1... | collective-permute-start | bytes 1572872 | tf_op jit(solution)/shard_map/ppermute | solution.py:336
  33.5 0.7 share_kept.1.kept_ref
  34.2 0.0 copy-done.6
  34.2 1.4 %rotate.1.turned_ref = bf16[16,144,128]{2,1,0:T(8,128)(2,1)S(1)} custom-call(bf16[16,288,128]{2,1,0:T(8,128)(2,1)S(1)} %all-to-all-done.got_ref, bf16[1024,1024]{1,0:T(8,128)(2,1)S(1)} %copy-done.6), custom_call_target="tpu_custom_call" | custom-call | flops 1000000000 | bytes 3866624 | tf_op jit(solution)/shard_map/rotate/pallas_call | solution.py:279
  35.7 0.0 collective-permute-done.taken_ref
  35.7 0.1 assemble.1
  35.8 0.0 copy-start.8
  35.8 0.0 copy-start.10
  35.8 20.5 %all_to_all.30.back_ref = bf16[16,272,128]{2,1,0:T(8,128)(2,1)S(1)} all-to-all(bf16[16,272,128]{2,1,0:T(8,128)(2,1)S(1)} %assemble.1), channel_id=1, replica_groups=mesh['site'=32,'mode'=16] {'mode'}, dimensions={0} | all-to-all | bytes 2228224 | tf_op jit(solution)/shard_map/all_to_all | solution.py:292
  56.3 0.1 sum_shares.1
  56.4 10.2 %all_to_all.31 = f32[4,8,512]{2,1,0:T(8,128)S(1)} all-to-all(f32[4,8,512]{2,1,0:T(8,128)S(1)} %sum_shares.1), channel_id=1, replica_groups={{0,32,64,96},{16,48,80,112},{128,160,192,224},{144,176,208,240},{256,28..., dimensions={0} | all-to-all | bytes 131072 | tf_op jit(solution)/shard_map/all_to_all | solution.py:292
  66.7 23.6 %all_to_all.32.far_ref = f32[4,8,512]{2,1,0:T(8,128)S(1)} all-to-all(f32[4,8,512]{2,1,0:T(8,128)S(1)} %broadcast_in_dim.4), channel_id=1, replica_groups={{0,128,256,384},{16,144,272,400},{32,160,288,416},{48,176,304,432},{64,..., dimensions={0} | all-to-all | bytes 131072 | tf_op jit(solution)/shard_map/all_to_all | solution.py:292
  90.3 0.0 copy-done.8
  90.3 0.0 copy-done.10
  90.3 0.0 copy-start.4
  90.3 0.4 project.1
  90.7 0.0 copy-start.2
  90.7 7.1 %all_to_all.33 = bf16[4,8,512]{2,1,0:T(8,128)(2,1)S(1)} all-to-all(bf16[4,8,512]{2,1,0:T(8,128)(2,1)S(1)} %convert), channel_id=1, replica_groups={{0,32,64,96},{16,48,80,112},{128,160,192,224},{144,176,208,240},{256,28..., dimensions={0} | all-to-all | bytes 65536 | tf_op jit(solution)/shard_map/all_to_all | solution.py:292
  97.9 11.7 %all_to_all.34.rows_ref = bf16[16,32,512]{2,1,0:T(8,128)(2,1)S(1)} all-to-all(bf16[16,32,512]{2,1,0:T(8,128)(2,1)S(1)} %broadcast_in_dim.5), channel_id=1, replica_groups=mesh['site'=32,'mode'=16] {'mode'}, dimensions={0} | all-to-all | bytes 1048576 | tf_op jit(solution)/shard_map/all_to_all | solution.py:292
  109.6 8.8 %collective-permute-start.1 = (bf16[16,32,512]{2,1,0:T(8,128)(2,1)S(1)}, bf16[16,32,512]{2,1,0:T(8,128)(2,1)S(1)}, u32[]{:S(2)}, u32[]{:S(2)}) collective-permute-start(bf16[16,32,512]{2,1,0:T(8,128)(2,1)S(1)} %all_to_all.34.rows_ref), channel_id=1, source_target_pairs={{0,16},{16,0},{32,48},{48,32},{64,80},{80,64},{96,112},{112,96},{1... | collective-permute-start | bytes 1572872 | tf_op jit(solution)/shard_map/ppermute | solution.py:356
  118.4 1.0 unpack.1
  119.3 0.0 copy-done.4
  119.3 0.0 copy-done.2
  119.3 1.2 %finish_own.1.first_ref = f32[2,512,512]{2,1,0:T(8,128)S(1)} custom-call(bf16[16,32,512]{2,1,0:T(8,128)(2,1)S(1)} %all_to_all.34.rows_ref, bf16[2,1024,512]{2,1,0:T(8,128)(2,1)S(1)} %copy-done.2, bf16[2,1024,512]{2,1,0:T(8,128)(2,1)S(1)} %copy-done.4), custom_call_target="tpu_custom_call" | custom-call | flops 1000000000 | bytes 6815744 | tf_op jit(solution)/shard_map/finish_own/pallas_call | solution.py:279
  120.6 0.0 collective-permute-done.1.rows_ref
  120.6 2.1 %finish_other.1 = f32[2,512,512]{2,1,0:T(8,128)} custom-call(bf16[16,32,512]{2,1,0:T(8,128)(2,1)S(1)} %collective-permute-done.1.rows_ref, bf16[2,1024,512]{2,1,0:T(8,128)(2,1)S(1)} %copy-done.2, bf16[2,1024,512]{2,1,0:T(8,128)(2,1)S(1)} %copy-done.4, f32[2,512,512]{2,1,0:T(8,128)S(1)} %finish_own.1.first_ref), custom_call_target="tpu_custom_call" | custom-call | flops 1000000000 | bytes 8912896 | tf_op jit(solution)/shard_map/finish_other/pallas_call | solution.py:279
  (4 shorter events, 0.1 us)
Async XLA Ops:
  0.6 10.1 %copy-start = (f32[2,512,512]{2,1,0:T(8,128)S(1)}, f32[2,512,512]{2,1,0:T(8,128)}, u32[]{:S(2)}) copy-start(f32[2,512,512]{2,1,0:T(8,128)} %ritz_ref.2) | copy-start | bytes 6291460
  3.1 23.6 %all-to-all-start = ((bf16[16,288,128]{2,1,0:T(8,128)(2,1)}), bf16[16,288,128]{2,1,0:T(8,128)(2,1)S(1)}, u32[]{:S(2)}, u32[]{:S(2)}) async-start(bf16[16,288,128]{2,1,0:T(8,128)(2,1)} %pack.1), calls=%async_computation | async-start | bytes 2359296 | tf_op jit(solution)/shard_map/all_to_all | solution.py:292
  11.2 1.3 %copy-start.5 = (bf16[1024,1024]{1,0:T(8,128)(2,1)}, bf16[1024,1024]{1,0:T(8,128)(2,1)S(1)}, u32[]{:S(2)}) copy-start(bf16[1024,1024]{1,0:T(8,128)(2,1)S(1)} %turn_matrix.1.turn_ref) | copy-start | bytes 6291460
  12.8 1.0 copy-start.7
  13.8 1.0 copy-start.9
  15.9 1.3 %copy-start.1 = (bf16[2,1024,512]{2,1,0:T(8,128)(2,1)}, bf16[2,1024,512]{2,1,0:T(8,128)(2,1)S(1)}, u32[]{:S(2)}) copy-start(bf16[2,1024,512]{2,1,0:T(8,128)(2,1)S(1)} %get-tuple-element.28.high_ref) | copy-start | bytes 6291460
  17.3 1.3 %copy-start.3 = (bf16[2,1024,512]{2,1,0:T(8,128)(2,1)}, bf16[2,1024,512]{2,1,0:T(8,128)(2,1)S(1)}, u32[]{:S(2)}) copy-start(bf16[2,1024,512]{2,1,0:T(8,128)(2,1)S(1)} %get-tuple-element.29.low_ref) | copy-start | bytes 6291460
  27.4 6.9 %copy-start.6 = (bf16[1024,1024]{1,0:T(8,128)(2,1)S(1)}, bf16[1024,1024]{1,0:T(8,128)(2,1)}, u32[]{:S(2)}) copy-start(bf16[1024,1024]{1,0:T(8,128)(2,1)} %copy-done.5) | copy-start | bytes 6291460
  27.4 8.3 %collective-permute-start = (bf16[16,128,128]{2,1,0:T(8,128)(2,1)S(1)}, bf16[16,128,128]{2,1,0:T(8,128)(2,1)S(1)}, u32[]{:S(2)}, u32[]{:S(2)}) collective-permute-start(bf16[16,128,128]{2,1,0:T(8,128)(2,1)S(1)} %share_given.1), channel_id=1, source_target_pairs={{0,16},{16,0},{32,48},{48,32},{64,80},{80,64},{96,112},{112,96},{1... | collective-permute-start | bytes 1572872 | tf_op jit(solution)/shard_map/ppermute | solution.py:336
  35.8 54.5 %copy-start.8 = (bf16[2,512,512]{2,1,0:T(8,128)(2,1)S(1)}, bf16[2,512,512]{2,1,0:T(8,128)(2,1)}, u32[]{:S(2)}) copy-start(bf16[2,512,512]{2,1,0:T(8,128)(2,1)} %copy-done.7) | copy-start | bytes 3145732
  35.8 54.5 %copy-start.10 = (bf16[2,512,512]{2,1,0:T(8,128)(2,1)S(1)}, bf16[2,512,512]{2,1,0:T(8,128)(2,1)}, u32[]{:S(2)}) copy-start(bf16[2,512,512]{2,1,0:T(8,128)(2,1)} %copy-done.9) | copy-start | bytes 3145732
  90.3 29.0 %copy-start.4 = (bf16[2,1024,512]{2,1,0:T(8,128)(2,1)S(1)}, bf16[2,1024,512]{2,1,0:T(8,128)(2,1)}, u32[]{:S(2)}) copy-start(bf16[2,1024,512]{2,1,0:T(8,128)(2,1)} %copy-done.3) | copy-start | bytes 6291460
  90.7 28.7 %copy-start.2 = (bf16[2,1024,512]{2,1,0:T(8,128)(2,1)S(1)}, bf16[2,1024,512]{2,1,0:T(8,128)(2,1)}, u32[]{:S(2)}) copy-start(bf16[2,1024,512]{2,1,0:T(8,128)(2,1)} %copy-done.1) | copy-start | bytes 6291460
  109.6 11.0 %collective-permute-start.1 = (bf16[16,32,512]{2,1,0:T(8,128)(2,1)S(1)}, bf16[16,32,512]{2,1,0:T(8,128)(2,1)S(1)}, u32[]{:S(2)}, u32[]{:S(2)}) collective-permute-start(bf16[16,32,512]{2,1,0:T(8,128)(2,1)S(1)} %all_to_all.34.rows_ref), channel_id=1, source_target_pairs={{0,16},{16,0},{32,48},{48,32},{64,80},{80,64},{96,112},{112,96},{1... | collective-permute-start | bytes 1572872 | tf_op jit(solution)/shard_map/ppermute | solution.py:356

commit v3 on v2

--- a/solution.py
+++ b/solution.py
@@ -26,7 +26,6 @@
 SHARE_ROWS = 8 * HALF
 CHUNKS = 4
 NEAR = 4
-ROWS = HALF // NEAR
 
 NT = (((1,), (1,)), ((), ()))
 
@@ -124,18 +123,12 @@
 
 
 def left_kernel(ritz_ref, left_high_ref, left_low_ref):
-    groups = (PEERS, 2, HALF // 8, 8, MODES)
-    first = lax.broadcasted_iota(jnp.int32, (PEERS, 8, MODES), 1) < ROWS
+    groups = (PEERS, 2, HALF, MODES)
     real, imag = ritz_ref[0].reshape(groups), ritz_ref[1].reshape(groups)
     for core in range(2):
         for part in range(2):
-            blocks = []
-            for pair in range(HALF // 8):
-                one, two = (real, imag) if part == 0 else (-imag, real)
-                one, two = one[:, core, pair], two[:, core, pair]
-                blocks.append(jnp.where(first, one, pltpu.roll(two, ROWS, 1)))
-                blocks.append(jnp.where(first, pltpu.roll(one, ROWS, 1), two))
-            values = jnp.concatenate(blocks, axis=1).reshape(MODES, MODES).T
+            one, two = (real, imag) if part == 0 else (-imag, real)
+            values = jnp.concatenate([one[:, core], two[:, core]], axis=1).reshape(MODES, MODES).T
             rows = slice(part * MODES, (part + 1) * MODES)
             left_high_ref[core, rows, :], left_low_ref[core, rows, :] = split(values)
 
@@ -215,31 +208,42 @@
     total = back_ref[0, 0:SHARE_ROWS, :].astype(F32)
     for peer in range(1, PEERS):
         total += back_ref[peer, 0:SHARE_ROWS, :].astype(F32)
+    total = total.astype(BF16)
     for part in range(2):
         for column in range(4):
             at = (part * 4 + column) * HALF
-            for near in range(NEAR):
-                out_ref[near, part * ROWS : (part + 1) * ROWS, column * LANES : (column + 1) * LANES] = total[
-                    at + near * ROWS : at + (near + 1) * ROWS, :
+            for copy in range(out_ref.shape[0]):
+                out_ref[copy, part * HALF : (part + 1) * HALF, column * LANES : (column + 1) * LANES] = total[
+                    at : at + HALF, :
                 ]
 
 
-def project_kernel(far_ref, high_ref, low_ref, out_ref):
-    total = far_ref[0]
-    for peer in range(1, far_ref.shape[0]):
-        total += far_ref[peer]
-    high, low = split(total)
-    both = jnp.concatenate([high.astype(F32), low.astype(F32)], axis=0).astype(BF16)
+def total_of(pieces_ref):
+    total = pieces_ref[0].astype(F32)
+    for peer in range(1, pieces_ref.shape[0]):
+        total += pieces_ref[peer].astype(F32)
+    return total
+
+
+def add_kernel(pieces_ref, out_ref):
+    total = total_of(pieces_ref).astype(BF16)
+    for copy in range(out_ref.shape[0]):
+        out_ref[copy] = total
+
+
+def project_kernel(pieces_ref, high_ref, low_ref, out_ref):
+    high, low = split(total_of(pieces_ref))
+    both = jnp.concatenate([high, low], axis=0)
     products = []
     for part in range(2):
         first = jnp.dot(both, high_ref[part], preferred_element_type=F32)
-        second = jnp.dot(both, low_ref[part], preferred_element_type=F32)
-        products.append(first[0 : 2 * ROWS] + first[2 * ROWS : 4 * ROWS] + second[0 : 2 * ROWS])
-    real = products[0][0:ROWS] - products[1][ROWS : 2 * ROWS]
-    imag = products[0][ROWS : 2 * ROWS] + products[1][0:ROWS]
-    rows = jnp.concatenate([real, imag], axis=0)
-    for near in range(NEAR):
-        out_ref[near] = rows
+        second = jnp.dot(high, low_ref[part], preferred_element_type=F32)
+        products.append(first[0:OWNED] + first[OWNED : 2 * OWNED] + second)
+    real = products[0][0:HALF] - products[1][HALF:OWNED]
+    imag = products[0][HALF:OWNED] + products[1][0:HALF]
+    rows = jnp.concatenate([real, imag], axis=0).astype(BF16)
+    for copy in range(out_ref.shape[0]):
+        out_ref[copy] = rows
 
 
 def finish_products(half, rows_ref, high_ref, low_ref, here):
@@ -292,14 +296,10 @@
     return lax.all_to_all(pieces, axis, 0, 0, axis_index_groups=groups)
 
 
-def spread(piece, count):
-    return jnp.broadcast_to(piece[None], (count,) + piece.shape)
-
-
 def on_device(site_count, vectors, images, ritz):
-    far = site_count // (2 * NEAR)
-    near_groups = [[2 * (NEAR * h + z) + c for z in range(NEAR)] for h in range(far) for c in range(2)]
-    far_groups = [[2 * (NEAR * h + z) + c for h in range(far)] for z in range(NEAR) for c in range(2)]
+    cores, steps = range(2), range(NEAR)
+    near_groups = [[[2 * (NEAR * h + z) + c for z in (3,2,1,0)] for h in steps] for c in cores]
+    far_groups = [[[2 * (NEAR * h + z) + c for h in (2,1,3,0)] for z in steps] for c in cores]
     swap = [(i, i ^ 1) for i in range(site_count)]
     width = PEERS * MAIN + 4 * LANES
     share = (PEERS, SHARE_ROWS, LANES)
@@ -346,12 +346,12 @@
     )
     sent = call(assemble_kernel, "assemble", [((PEERS, SHARE_ROWS + PIECE_ROWS, LANES), BF16)], kept, taken, turned)
     back = exchange(sent, "mode")
-    summed = call(sum_kernel, "sum_shares", [((NEAR, 2 * ROWS, MODES), F32)], back)
-    summed = exchange(summed, "site", near_groups)
-    summed = exchange(spread(jnp.sum(summed, axis=0), far), "site", far_groups)
-    rows = call(project_kernel, "project", [((NEAR, 2 * ROWS, MODES), F32)], summed, *ritz_split)
-    rows = exchange(rows, "site", near_groups).reshape(OWNED, MODES).astype(BF16)
-    own = exchange(spread(rows, PEERS), "mode")
+    summed = call(sum_kernel, "sum_shares", [((NEAR, OWNED, MODES), BF16)], back)
+    summed = exchange(summed, "site", near_groups[0] + far_groups[1])
+    summed = call(add_kernel, "add_shares", [((NEAR, OWNED, MODES), BF16)], summed)
+    summed = exchange(summed, "site", far_groups[0] + near_groups[1])
+    rows = call(project_kernel, "project", [((PEERS, OWNED, MODES), BF16)], summed, *ritz_split)
+    own = exchange(rows, "mode")
     own, back = lax.optimization_barrier((own, back))
     other = lax.ppermute(own, "site", swap)
     rotated = call(unpack_kernel, "unpack", local, back)

time: 123 us -> 108 us (0.88)
  blocking collectives: 73.2 us -> 60.5 us
  starting transfers between devices: 22.5 us -> 20.2 us
    all_to_all x5 -> x4, blocking collectives: 73.2 us -> 60.5 us  [exchange(): return lax.all_to_all(pieces, axis, 0, 0, axis_index_groups=groups)]
    ppermute x1, starting transfers between devices: 8.77 us -> 6.5 us  [on_device(): other = lax.ppermute(own, 'site', swap)]
    pallas_call x13 -> x14, Pallas kernels: 12 us -> 12.1 us  [call(): pl.pallas_call(kernel, name=name, out_shape=outs[0] if single else outs,...]
  transfers between devices with their start and end apart: 3 -> 3, of which waited for: 1 -> 1; matrix products, arithmetic and copies ran while one was open for 0% -> 0% of each run, Pallas kernels for 5% -> 6%
where the time goes in v3:
time: 108 us
  blocking collectives  60.5 us (56%)
  starting transfers between devices  20.2 us (19%)
  Pallas kernels  12.1 us (11%)
  waiting for transfers between devices  8.1 us (8%)
  local copies, waits for them, and re-layouts  5.94 us (6%)
    all_to_all x4, blocking collectives, exchange(): return lax.all_to_all(pieces, axis, 0, 0, axis_index_groups=groups)  60.5 us
    pallas_call x14, Pallas kernels, call(): pl.pallas_call(kernel, name=name, out_shape=outs[0] if single else outs,...  12.1 us
    all_to_all x1, waiting for transfers between devices, exchange(): return lax.all_to_all(pieces, axis, 0, 0, axis_index_groups=groups)  8.09 us
    all_to_all x1, starting transfers between devices, exchange(): return lax.all_to_all(pieces, axis, 0, 0, axis_index_groups=groups)  7.6 us
    ppermute x1, starting transfers between devices, on_device(): other = lax.ppermute(own, 'site', swap)  6.5 us
    ppermute x1, starting transfers between devices, on_device(): taken = lax.ppermute(given, 'site', swap)  6.15 us
    unnamed x22, local copies, waits for them, and re-layouts  5.94 us
  transfers between devices with their start and end apart: 3, of which 1 were waited for; matrix products, arithmetic and copies ran while one was open for 0% of the time, Pallas kernels for 6%

profile of v3, /device:TPU:1, one launch (start us, length us, event | category | flops | bytes accessed | tf_op | source)
XLA Modules:
  0.0 107.8 jit_solution(4007090285104921448)
XLA Ops:
  0.6 0.0 copy-start
  0.6 2.4 %pack.1 = bf16[16,288,128]{2,1,0:T(8,128)(2,1)} custom-call(bf16[2,32,4608]{2,1,0:T(8,128)(2,1)} %vectors_hbm.1, bf16[2,32,4608]{2,1,0:T(8,128)(2,1)} %images_hbm.1), custom_call_target="tpu_custom_call" | custom-call | bytes 2359296 | tf_op jit(solution)/shard_map/pack/pallas_call | solution.py:283
  3.1 7.6 %all-to-all-start = ((bf16[16,288,128]{2,1,0:T(8,128)(2,1)}), bf16[16,288,128]{2,1,0:T(8,128)(2,1)S(1)}, u32[]{:S(2)}, u32[]{:S(2)}) async-start(bf16[16,288,128]{2,1,0:T(8,128)(2,1)} %pack.1), calls=%async_computation | async-start | bytes 2359296 | tf_op jit(solution)/shard_map/all_to_all | solution.py:296
  10.7 0.0 copy-done
  10.7 0.5 turn_matrix.1.turn_ref
  11.2 0.0 copy-start.5
  11.2 1.3 %copy-done.5 = bf16[1024,1024]{1,0:T(8,128)(2,1)} copy-done((bf16[1024,1024]{1,0:T(8,128)(2,1)}, bf16[1024,1024]{1,0:T(8,128)(2,1)S(1)}, u32[]{:S(2)}) %copy-start.5) | copy-done | bytes 2097176
  12.5 0.3 split_ritz.1
  12.8 0.0 copy-start.7
  12.8 1.0 copy-done.7
  13.8 0.0 copy-start.9
  13.8 1.0 copy-done.9
  14.7 1.1 %left_factors.1 = (bf16[2,1024,512]{2,1,0:T(8,128)(2,1)S(1)}, bf16[2,1024,512]{2,1,0:T(8,128)(2,1)S(1)}) custom-call(f32[2,512,512]{2,1,0:T(8,128)S(1)} %copy-done), custom_call_target="tpu_custom_call" | custom-call | bytes 6291456 | tf_op jit(solution)/shard_map/left_factors/pallas_call | solution.py:283
  15.9 0.0 copy-start.1
  15.9 1.3 %copy-done.1 = bf16[2,1024,512]{2,1,0:T(8,128)(2,1)} copy-done((bf16[2,1024,512]{2,1,0:T(8,128)(2,1)}, bf16[2,1024,512]{2,1,0:T(8,128)(2,1)S(1)}, u32[]{:S(2)}) %copy-start.1) | copy-done | bytes 2097176
  17.2 0.0 copy-start.3
  17.2 1.3 %copy-done.3 = bf16[2,1024,512]{2,1,0:T(8,128)(2,1)} copy-done((bf16[2,1024,512]{2,1,0:T(8,128)(2,1)}, bf16[2,1024,512]{2,1,0:T(8,128)(2,1)S(1)}, u32[]{:S(2)}) %copy-start.3) | copy-done | bytes 2097176
  18.6 8.1 %all-to-all-done.got_ref = bf16[16,288,128]{2,1,0:T(8,128)(2,1)S(1)} async-done(((bf16[16,288,128]{2,1,0:T(8,128)(2,1)}), bf16[16,288,128]{2,1,0:T(8,128)(2,1)S(1)}, u32[]{:S(2)}, u32[]{:S(2)}) %all-to-all-start) | async-done | bytes 1179680 | tf_op jit(solution)/shard_map/all_to_all | solution.py:296
  26.7 0.7 share_given.1
  27.4 0.0 copy-start.6
  27.4 6.2 %collective-permute-start = (bf16[16,128,128]{2,1,0:T(8,128)(2,1)S(1)}, bf16[16,128,128]{2,1,0:T(8,128)(2,1)S(1)}, u32[]{:S(2)}, u32[]{:S(2)}) collective-permute-start(bf16[16,128,128]{2,1,0:T(8,128)(2,1)S(1)} %share_given.1), channel_id=1, source_target_pairs={{0,16},{16,0},{32,48},{48,32},{64,80},{80,64},{96,112},{112,96},{1... | collective-permute-start | bytes 1572872 | tf_op jit(solution)/shard_map/ppermute | solution.py:336
  33.5 0.7 share_kept.1.kept_ref
  34.2 0.0 copy-done.6
  34.3 1.4 %rotate.1.turned_ref = bf16[16,144,128]{2,1,0:T(8,128)(2,1)S(1)} custom-call(bf16[16,288,128]{2,1,0:T(8,128)(2,1)S(1)} %all-to-all-done.got_ref, bf16[1024,1024]{1,0:T(8,128)(2,1)S(1)} %copy-done.6), custom_call_target="tpu_custom_call" | custom-call | flops 1000000000 | bytes 3866624 | tf_op jit(solution)/shard_map/rotate/pallas_call | solution.py:283
  35.7 0.0 collective-permute-done.taken_ref
  35.7 0.1 assemble.1
  35.8 0.0 copy-start.8
  35.8 0.0 copy-start.10
  35.8 20.5 %all_to_all.25.back_ref = bf16[16,272,128]{2,1,0:T(8,128)(2,1)S(1)} all-to-all(bf16[16,272,128]{2,1,0:T(8,128)(2,1)S(1)} %assemble.1), channel_id=1, replica_groups=mesh['site'=32,'mode'=16] {'mode'}, dimensions={0} | all-to-all | bytes 2228224 | tf_op jit(solution)/shard_map/all_to_all | solution.py:296
  56.3 0.1 sum_shares.1
  56.4 19.2 %all_to_all.26.pieces_ref = bf16[4,32,512]{2,1,0:T(8,128)(2,1)S(1)} all-to-all(bf16[4,32,512]{2,1,0:T(8,128)(2,1)S(1)} %sum_shares.1), channel_id=1, replica_groups={{96,64,32,0},{224,192,160,128},{352,320,288,256},{480,448,416,384},{272..., dimensions={0} | all-to-all | bytes 262144 | tf_op jit(solution)/shard_map/all_to_all | solution.py:296
  75.7 8.7 %all_to_all.27.pieces_ref = bf16[4,32,512]{2,1,0:T(8,128)(2,1)S(1)} all-to-all(bf16[4,32,512]{2,1,0:T(8,128)(2,1)S(1)} %add_shares.1), channel_id=1, replica_groups={{256,128,384,0},{288,160,416,32},{320,192,448,64},{352,224,480,96},{112..., dimensions={0} | all-to-all | bytes 262144 | tf_op jit(solution)/shard_map/all_to_all | solution.py:296
  84.4 0.0 copy-done.8
  84.4 0.0 copy-done.10
  84.4 0.0 copy-start.2
  84.4 0.0 copy-start.4
  84.4 0.5 project.1
  84.9 12.1 %all_to_all.28.rows_ref = bf16[16,32,512]{2,1,0:T(8,128)(2,1)S(1)} all-to-all(bf16[16,32,512]{2,1,0:T(8,128)(2,1)S(1)} %project.1), channel_id=1, replica_groups=mesh['site'=32,'mode'=16] {'mode'}, dimensions={0} | all-to-all | bytes 1048576 | tf_op jit(solution)/shard_map/all_to_all | solution.py:296
  97.0 6.5 %collective-permute-start.1 = (bf16[16,32,512]{2,1,0:T(8,128)(2,1)S(1)}, bf16[16,32,512]{2,1,0:T(8,128)(2,1)S(1)}, u32[]{:S(2)}, u32[]{:S(2)}) collective-permute-start(bf16[16,32,512]{2,1,0:T(8,128)(2,1)S(1)} %all_to_all.28.rows_ref), channel_id=1, source_target_pairs={{0,16},{16,0},{32,48},{48,32},{64,80},{80,64},{96,112},{112,96},{1... | collective-permute-start | bytes 1572872 | tf_op jit(solution)/shard_map/ppermute | solution.py:356
  103.5 1.0 unpack.1
  104.4 0.0 copy-done.2
  104.4 0.0 copy-done.4
  104.4 1.2 %finish_own.1.first_ref = f32[2,512,512]{2,1,0:T(8,128)S(1)} custom-call(bf16[16,32,512]{2,1,0:T(8,128)(2,1)S(1)} %all_to_all.28.rows_ref, bf16[2,1024,512]{2,1,0:T(8,128)(2,1)S(1)} %copy-done.2, bf16[2,1024,512]{2,1,0:T(8,128)(2,1)S(1)} %copy-done.4), custom_call_target="tpu_custom_call" | custom-call | flops 1000000000 | bytes 6815744 | tf_op jit(solution)/shard_map/finish_own/pallas_call | solution.py:283
  105.7 0.0 collective-permute-done.1.rows_ref
  105.7 2.1 %finish_other.1 = f32[2,512,512]{2,1,0:T(8,128)} custom-call(bf16[16,32,512]{2,1,0:T(8,128)(2,1)S(1)} %collective-permute-done.1.rows_ref, bf16[2,1024,512]{2,1,0:T(8,128)(2,1)S(1)} %copy-done.2, bf16[2,1024,512]{2,1,0:T(8,128)(2,1)S(1)} %copy-done.4, f32[2,512,512]{2,1,0:T(8,128)S(1)} %finish_own.1.first_ref), custom_call_target="tpu_custom_call" | custom-call | flops 1000000000 | bytes 8912896 | tf_op jit(solution)/shard_map/finish_other/pallas_call | solution.py:283
  (1 shorter events, 0.0 us)
Async XLA Ops:
  0.6 10.1 %copy-start = (f32[2,512,512]{2,1,0:T(8,128)S(1)}, f32[2,512,512]{2,1,0:T(8,128)}, u32[]{:S(2)}) copy-start(f32[2,512,512]{2,1,0:T(8,128)} %ritz_ref.2) | copy-start | bytes 6291460
  3.1 23.6 %all-to-all-start = ((bf16[16,288,128]{2,1,0:T(8,128)(2,1)}), bf16[16,288,128]{2,1,0:T(8,128)(2,1)S(1)}, u32[]{:S(2)}, u32[]{:S(2)}) async-start(bf16[16,288,128]{2,1,0:T(8,128)(2,1)} %pack.1), calls=%async_computation | async-start | bytes 2359296 | tf_op jit(solution)/shard_map/all_to_all | solution.py:296
  11.2 1.3 %copy-start.5 = (bf16[1024,1024]{1,0:T(8,128)(2,1)}, bf16[1024,1024]{1,0:T(8,128)(2,1)S(1)}, u32[]{:S(2)}) copy-start(bf16[1024,1024]{1,0:T(8,128)(2,1)S(1)} %turn_matrix.1.turn_ref) | copy-start | bytes 6291460
  12.8 1.0 copy-start.7
  13.8 1.0 copy-start.9
  15.9 1.3 %copy-start.1 = (bf16[2,1024,512]{2,1,0:T(8,128)(2,1)}, bf16[2,1024,512]{2,1,0:T(8,128)(2,1)S(1)}, u32[]{:S(2)}) copy-start(bf16[2,1024,512]{2,1,0:T(8,128)(2,1)S(1)} %get-tuple-element.28.high_ref) | copy-start | bytes 6291460
  17.2 1.3 %copy-start.3 = (bf16[2,1024,512]{2,1,0:T(8,128)(2,1)}, bf16[2,1024,512]{2,1,0:T(8,128)(2,1)S(1)}, u32[]{:S(2)}) copy-start(bf16[2,1024,512]{2,1,0:T(8,128)(2,1)S(1)} %get-tuple-element.29.low_ref) | copy-start | bytes 6291460
  27.4 6.9 %copy-start.6 = (bf16[1024,1024]{1,0:T(8,128)(2,1)S(1)}, bf16[1024,1024]{1,0:T(8,128)(2,1)}, u32[]{:S(2)}) copy-start(bf16[1024,1024]{1,0:T(8,128)(2,1)} %copy-done.5) | copy-start | bytes 6291460
  27.4 8.3 %collective-permute-start = (bf16[16,128,128]{2,1,0:T(8,128)(2,1)S(1)}, bf16[16,128,128]{2,1,0:T(8,128)(2,1)S(1)}, u32[]{:S(2)}, u32[]{:S(2)}) collective-permute-start(bf16[16,128,128]{2,1,0:T(8,128)(2,1)S(1)} %share_given.1), channel_id=1, source_target_pairs={{0,16},{16,0},{32,48},{48,32},{64,80},{80,64},{96,112},{112,96},{1... | collective-permute-start | bytes 1572872 | tf_op jit(solution)/shard_map/ppermute | solution.py:336
  35.8 48.6 %copy-start.8 = (bf16[2,512,512]{2,1,0:T(8,128)(2,1)S(1)}, bf16[2,512,512]{2,1,0:T(8,128)(2,1)}, u32[]{:S(2)}) copy-start(bf16[2,512,512]{2,1,0:T(8,128)(2,1)} %copy-done.7) | copy-start | bytes 3145732
  35.8 48.6 %copy-start.10 = (bf16[2,512,512]{2,1,0:T(8,128)(2,1)S(1)}, bf16[2,512,512]{2,1,0:T(8,128)(2,1)}, u32[]{:S(2)}) copy-start(bf16[2,512,512]{2,1,0:T(8,128)(2,1)} %copy-done.9) | copy-start | bytes 3145732
  84.4 20.1 %copy-start.2 = (bf16[2,1024,512]{2,1,0:T(8,128)(2,1)S(1)}, bf16[2,1024,512]{2,1,0:T(8,128)(2,1)}, u32[]{:S(2)}) copy-start(bf16[2,1024,512]{2,1,0:T(8,128)(2,1)} %copy-done.1) | copy-start | bytes 6291460
  84.4 20.1 %copy-start.4 = (bf16[2,1024,512]{2,1,0:T(8,128)(2,1)S(1)}, bf16[2,1024,512]{2,1,0:T(8,128)(2,1)}, u32[]{:S(2)}) copy-start(bf16[2,1024,512]{2,1,0:T(8,128)(2,1)} %copy-done.3) | copy-start | bytes 6291460
  97.0 8.7 %collective-permute-start.1 = (bf16[16,32,512]{2,1,0:T(8,128)(2,1)S(1)}, bf16[16,32,512]{2,1,0:T(8,128)(2,1)S(1)}, u32[]{:S(2)}, u32[]{:S(2)}) collective-permute-start(bf16[16,32,512]{2,1,0:T(8,128)(2,1)S(1)} %all_to_all.28.rows_ref), channel_id=1, source_target_pairs={{0,16},{16,0},{32,48},{48,32},{64,80},{80,64},{96,112},{112,96},{1... | collective-permute-start | bytes 1572872 | tf_op jit(solution)/shard_map/ppermute | solution.py:356

commit v4 on v3

--- a/solution.py
+++ b/solution.py
@@ -24,8 +24,10 @@
 PIECE_ROWS = TAIL_ROW + HALF
 DEPTH = 2 * MAIN + LANES
 SHARE_ROWS = 8 * HALF
-CHUNKS = 4
+CHUNKS = 2
 NEAR = 4
+
+REVERSED = list(range(PEERS))[::-1]
 
 NT = (((1,), (1,)), ((), ()))
 
@@ -64,8 +66,8 @@
                         at = peer * MAIN + block * LANES
                         for part in range(2):
                             row = base + (block * 2 + part) * OWNED
-                            out_ref[peer, row : row + OWNED, :] = source_ref[part, :, at : at + LANES]
-                where = (pl.ds(chunk * peers, peers), pl.ds(base, TAIL_ROW))
+                            out_ref[REVERSED[peer], row : row + OWNED, :] = source_ref[part, :, at : at + LANES]
+                where = (pl.ds(PEERS - (chunk + 1) * peers, peers), pl.ds(base, TAIL_ROW))
             else:
                 for block in range(PEERS // 4):
                     at = TAIL_AT + block * LANES
@@ -78,7 +80,7 @@
                         packed = turn(tails[0], -quarter)
                         for slot in range(1, 4):
                             packed = jnp.where(group == slot, turn(tails[slot], slot - quarter), packed)
-                        out_ref[block * 4 + quarter, base + TAIL_ROW : base + PIECE_ROWS, :] = packed.astype(BF16)
+                        out_ref[REVERSED[block * 4 + quarter], base + TAIL_ROW : base + PIECE_ROWS, :] = packed.astype(BF16)
                 where = (pl.ds(0, PEERS), pl.ds(base + TAIL_ROW, HALF))
             copy = pltpu.make_async_copy(out_ref.at[where], out_hbm.at[where], sent.at[index])
             copy.start()
@@ -87,16 +89,25 @@
         copy.wait()
 
 
+def of_owners(got_ref, rows):
+    return jnp.concatenate([got_ref[at, rows, :] for at in REVERSED], axis=0)
+
+
+def tails_of(got_ref, base):
+    values = of_owners(got_ref, slice(base + TAIL_ROW, base + PIECE_ROWS)).astype(F32)
+    return values.reshape(PEERS, HALF, LANES)
+
+
 def unpack_kernel(back_ref, out_ref):
     for peer in range(PEERS):
         for block in range(2):
             at = peer * MAIN + block * LANES
             for part in range(2):
                 row = SHARE_ROWS + (block * 2 + part) * OWNED
-                out_ref[part, :, at : at + LANES] = back_ref[peer, row : row + OWNED, :]
+                out_ref[part, :, at : at + LANES] = back_ref[REVERSED[peer], row : row + OWNED, :]
     group = lane_group((HALF, LANES))
     for block in range(PEERS // 4):
-        ends = [back_ref[block * 4 + quarter, SHARE_ROWS + TAIL_ROW : SHARE_ROWS + PIECE_ROWS, :].astype(F32) for quarter in range(4)]
+        ends = [back_ref[REVERSED[block * 4 + quarter], SHARE_ROWS + TAIL_ROW : SHARE_ROWS + PIECE_ROWS, :].astype(F32) for quarter in range(4)]
         at = TAIL_AT + block * LANES
         for slot in range(4):
             values = turn(ends[0], -slot)
@@ -128,25 +139,25 @@
     for core in range(2):
         for part in range(2):
             one, two = (real, imag) if part == 0 else (-imag, real)
-            values = jnp.concatenate([one[:, core], two[:, core]], axis=1).reshape(MODES, MODES).T
+            values = jnp.concatenate([side[owner, core] for owner in REVERSED for side in (one, two)], axis=0).T
             rows = slice(part * MODES, (part + 1) * MODES)
             left_high_ref[core, rows, :], left_low_ref[core, rows, :] = split(values)
 
 
 def rotate_kernel(got_ref, turn_ref, out_ref, stacked):
-    packed = got_ref[:, TAIL_ROW:PIECE_ROWS, :].astype(F32)
+    packed = tails_of(got_ref, 0)
     for part in range(2):
         rows = slice(part * MODES, (part + 1) * MODES)
         for block in range(2):
             at = (block * 2 + part) * OWNED
-            stacked[rows, block * LANES : (block + 1) * LANES] = got_ref[:, at : at + OWNED, :].reshape(MODES, LANES)
+            stacked[rows, block * LANES : (block + 1) * LANES] = of_owners(got_ref, slice(at, at + OWNED))
         ends = jnp.concatenate([turn(packed, -2 * part), turn(packed, -2 * part - 1)], axis=1)
         stacked[rows, MAIN : MAIN + LANES] = ends.reshape(MODES, LANES).astype(BF16)
 
     owners = HALF_MODES // OWNED
     group = lane_group((owners, HALF, LANES))
     for step in range(2):
-        peers = slice(step * owners, (step + 1) * owners)
+        places = REVERSED[step * owners : (step + 1) * owners]
         sent = None
         for part in range(2):
             at = part * MODES + step * HALF_MODES
@@ -154,12 +165,14 @@
             for block in range(2):
                 row = (block * 2 + part) * OWNED
                 values = rotated[:, block * LANES : (block + 1) * LANES].astype(BF16)
-                out_ref[peers, row : row + OWNED, :] = values.reshape(owners, OWNED, LANES)
+                for owner, place in enumerate(places):
+                    out_ref[place, row : row + OWNED, :] = values[owner * OWNED : (owner + 1) * OWNED, :]
             ends = rotated[:, MAIN : MAIN + LANES].reshape(owners, OWNED, LANES)
             for half in range(2):
                 moved = turn(ends[:, half * HALF : (half + 1) * HALF, :], part * 2 + half)
                 sent = moved if sent is None else jnp.where(group == part * 2 + half, moved, sent)
-        out_ref[peers, TAIL_ROW:PIECE_ROWS, :] = sent.astype(BF16)
+        for owner, place in enumerate(places):
+            out_ref[place, TAIL_ROW:PIECE_ROWS, :] = sent[owner].astype(BF16)
 
 
 def share_kernel(other, got_ref, out_ref, left, right):
@@ -180,13 +193,13 @@
     ends = jnp.where(half == 0, side(packed, 0, (0, 1), (1, 1)), side(packed, 1, (0, 1), (1, 1)))
     left[:, 2 * MAIN : DEPTH] = ends.reshape(HALF_MODES, LANES).astype(BF16)
 
-    packed = got_ref[:, PIECE_ROWS + TAIL_ROW : 2 * PIECE_ROWS, :].astype(F32)
+    packed = tails_of(got_ref, PIECE_ROWS)
     for part in range(2):
         sources, signs = ((0, 1), (1, 1)) if part == 0 else ((1, 0), (1, -1))
         for place in range(2):
             for block in range(2):
                 at = PIECE_ROWS + (block * 2 + sources[place]) * OWNED
-                values = got_ref[:, at : at + OWNED, :].reshape(MODES, LANES)
+                values = of_owners(got_ref, slice(at, at + OWNED))
                 lanes = slice(place * MAIN + block * LANES, place * MAIN + (block + 1) * LANES)
                 right[part, :, lanes] = values if signs[place] > 0 else -values
         ends = jnp.concatenate([side(packed, row_half, sources, signs) for row_half in range(2)], axis=1)
@@ -329,7 +342,7 @@
         call(left_kernel, "left_factors", [((2, 2 * MODES, MODES), BF16)] * 2, ritz),
         call(split_kernel, "split_ritz", [(ritz.shape, BF16)] * 2, ritz),
     )
-    got, (turn_matrix, left, ritz_split) = lax.optimization_barrier((exchange(packed, "mode"), factors))
+    got, (turn_matrix, left, ritz_split) = lax.optimization_barrier((exchange(packed, "mode", [REVERSED]), factors))
 
     sides = [pltpu.VMEM((HALF_MODES, DEPTH), BF16), pltpu.VMEM((2, MODES, DEPTH), BF16)]
     given = call(functools.partial(share_kernel, True), "share_given", [(share, BF16)], got, flops=10**9, scratch=sides)
@@ -345,13 +358,13 @@
         scratch=[pltpu.VMEM((2 * MODES, MAIN + LANES), BF16)],
     )
     sent = call(assemble_kernel, "assemble", [((PEERS, SHARE_ROWS + PIECE_ROWS, LANES), BF16)], kept, taken, turned)
-    back = exchange(sent, "mode")
+    back = exchange(sent, "mode", [REVERSED])
     summed = call(sum_kernel, "sum_shares", [((NEAR, OWNED, MODES), BF16)], back)
     summed = exchange(summed, "site", near_groups[0] + far_groups[1])
     summed = call(add_kernel, "add_shares", [((NEAR, OWNED, MODES), BF16)], summed)
     summed = exchange(summed, "site", far_groups[0] + near_groups[1])
     rows = call(project_kernel, "project", [((PEERS, OWNED, MODES), BF16)], summed, *ritz_split)
-    own = exchange(rows, "mode")
+    own = exchange(rows, "mode", [REVERSED])
     own, back = lax.optimization_barrier((own, back))
     other = lax.ppermute(own, "site", swap)
     rotated = call(unpack_kernel, "unpack", local, back)

time: 108 us -> 107 us (level)
  waiting for transfers between devices: 8.1 us -> 4.12 us
  starting transfers between devices: 20.2 us -> 22.4 us
    all_to_all x1, waiting for transfers between devices: 8.09 us -> 4.11 us  [exchange(): return lax.all_to_all(pieces, axis, 0, 0, axis_index_groups=groups)]
    all_to_all x1, starting transfers between devices: 7.6 us -> 9.35 us  [exchange(): return lax.all_to_all(pieces, axis, 0, 0, axis_index_groups=groups)]
where the time goes in v4:
time: 107 us; the launch traced here: 106 us
  blocking collectives  60.6 us (57%)
  starting transfers between devices  22.4 us (21%)
  Pallas kernels  12.2 us (11%)
  local copies, waits for them, and re-layouts  5.94 us (6%)
  waiting for transfers between devices  4.12 us (4%)
    all_to_all x4, blocking collectives, exchange(): return lax.all_to_all(pieces, axis, 0, 0, axis_index_groups=groups)  60.6 us
    pallas_call x14, Pallas kernels, call(): pl.pallas_call(kernel, name=name, out_shape=outs[0] if single else outs,...  12.2 us
    all_to_all x1, starting transfers between devices, exchange(): return lax.all_to_all(pieces, axis, 0, 0, axis_index_groups=groups)  9.35 us
    ppermute x1, starting transfers between devices, on_device(): other = lax.ppermute(own, 'site', swap)  6.79 us
    ppermute x1, starting transfers between devices, on_device(): taken = lax.ppermute(given, 'site', swap)  6.21 us
    unnamed x22, local copies, waits for them, and re-layouts  5.94 us
    all_to_all x1, waiting for transfers between devices, exchange(): return lax.all_to_all(pieces, axis, 0, 0, axis_index_groups=groups)  4.11 us
  transfers between devices with their start and end apart: 3, of which 1 were waited for; matrix products, arithmetic and copies ran while one was open for 0% of the time, Pallas kernels for 6%

profile of v4, /device:TPU:1, one launch (start us, length us, event | category | flops | bytes accessed | tf_op | source)
XLA Modules:
  0.0 106.0 jit_solution(2417772607239787785)
XLA Ops:
  0.6 0.0 copy-start
  0.6 2.3 %pack.1 = bf16[16,288,128]{2,1,0:T(8,128)(2,1)} custom-call(bf16[2,32,4608]{2,1,0:T(8,128)(2,1)} %vectors_hbm.1, bf16[2,32,4608]{2,1,0:T(8,128)(2,1)} %images_hbm.1), custom_call_target="tpu_custom_call" | custom-call | bytes 2359296 | tf_op jit(solution)/shard_map/pack/pallas_call | solution.py:296
  3.0 9.4 %all-to-all-start = ((bf16[16,288,128]{2,1,0:T(8,128)(2,1)}), bf16[16,288,128]{2,1,0:T(8,128)(2,1)S(1)}, u32[]{:S(2)}, u32[]{:S(2)}) async-start(bf16[16,288,128]{2,1,0:T(8,128)(2,1)} %pack.1), calls=%async_computation | async-start | bytes 2359296 | tf_op jit(solution)/shard_map/all_to_all | solution.py:309
  12.3 0.0 copy-done
  12.3 0.5 turn_matrix.1.turn_ref
  12.8 0.0 copy-start.5
  12.8 1.3 %copy-done.5 = bf16[1024,1024]{1,0:T(8,128)(2,1)} copy-done((bf16[1024,1024]{1,0:T(8,128)(2,1)}, bf16[1024,1024]{1,0:T(8,128)(2,1)S(1)}, u32[]{:S(2)}) %copy-start.5) | copy-done | bytes 2097176
  14.1 0.3 split_ritz.1
  14.4 0.0 copy-start.7
  14.4 1.0 copy-done.7
  15.4 0.0 copy-start.9
  15.4 1.0 copy-done.9
  16.4 1.1 %left_factors.1 = (bf16[2,1024,512]{2,1,0:T(8,128)(2,1)S(1)}, bf16[2,1024,512]{2,1,0:T(8,128)(2,1)S(1)}) custom-call(f32[2,512,512]{2,1,0:T(8,128)S(1)} %copy-done), custom_call_target="tpu_custom_call" | custom-call | bytes 6291456 | tf_op jit(solution)/shard_map/left_factors/pallas_call | solution.py:296
  17.5 0.0 copy-start.1
  17.5 1.3 %copy-done.1 = bf16[2,1024,512]{2,1,0:T(8,128)(2,1)} copy-done((bf16[2,1024,512]{2,1,0:T(8,128)(2,1)}, bf16[2,1024,512]{2,1,0:T(8,128)(2,1)S(1)}, u32[]{:S(2)}) %copy-start.1) | copy-done | bytes 2097176
  18.9 0.0 copy-start.3
  18.9 1.3 %copy-done.3 = bf16[2,1024,512]{2,1,0:T(8,128)(2,1)} copy-done((bf16[2,1024,512]{2,1,0:T(8,128)(2,1)}, bf16[2,1024,512]{2,1,0:T(8,128)(2,1)S(1)}, u32[]{:S(2)}) %copy-start.3) | copy-done | bytes 2097176
  20.2 4.1 %all-to-all-done.got_ref = bf16[16,288,128]{2,1,0:T(8,128)(2,1)S(1)} async-done(((bf16[16,288,128]{2,1,0:T(8,128)(2,1)}), bf16[16,288,128]{2,1,0:T(8,128)(2,1)S(1)}, u32[]{:S(2)}, u32[]{:S(2)}) %all-to-all-start) | async-done | bytes 1179680 | tf_op jit(solution)/shard_map/all_to_all | solution.py:309
  24.3 0.7 share_given.1
  25.1 0.0 copy-start.6
  25.1 6.2 %collective-permute-start = (bf16[16,128,128]{2,1,0:T(8,128)(2,1)S(1)}, bf16[16,128,128]{2,1,0:T(8,128)(2,1)S(1)}, u32[]{:S(2)}, u32[]{:S(2)}) collective-permute-start(bf16[16,128,128]{2,1,0:T(8,128)(2,1)S(1)} %share_given.1), channel_id=1, source_target_pairs={{0,16},{16,0},{32,48},{48,32},{64,80},{80,64},{96,112},{112,96},{1... | collective-permute-start | bytes 1572872 | tf_op jit(solution)/shard_map/ppermute | solution.py:349
  31.3 0.7 share_kept.1.kept_ref
  32.0 0.0 copy-done.6
  32.0 1.4 %rotate.1.turned_ref = bf16[16,144,128]{2,1,0:T(8,128)(2,1)S(1)} custom-call(bf16[16,288,128]{2,1,0:T(8,128)(2,1)S(1)} %all-to-all-done.got_ref, bf16[1024,1024]{1,0:T(8,128)(2,1)S(1)} %copy-done.6), custom_call_target="tpu_custom_call" | custom-call | flops 1000000000 | bytes 3866624 | tf_op jit(solution)/shard_map/rotate/pallas_call | solution.py:296
  33.5 0.0 collective-permute-done.taken_ref
  33.5 0.1 assemble.1
  33.6 0.0 copy-start.8
  33.6 0.0 copy-start.10
  33.6 21.1 %all_to_all.25.back_ref = bf16[16,272,128]{2,1,0:T(8,128)(2,1)S(1)} all-to-all(bf16[16,272,128]{2,1,0:T(8,128)(2,1)S(1)} %assemble.1), channel_id=1, replica_groups={{15,14,13,12,11,10,9,8,7,6,5,4,3,2,1,0},{31,30,29,28,27,26,25,24,23,22,..., dimensions={0} | all-to-all | bytes 2228224 | tf_op jit(solution)/shard_map/all_to_all | solution.py:309
  54.7 0.1 sum_shares.1
  54.8 19.2 %all_to_all.26.pieces_ref = bf16[4,32,512]{2,1,0:T(8,128)(2,1)S(1)} all-to-all(bf16[4,32,512]{2,1,0:T(8,128)(2,1)S(1)} %sum_shares.1), channel_id=1, replica_groups={{96,64,32,0},{224,192,160,128},{352,320,288,256},{480,448,416,384},{272..., dimensions={0} | all-to-all | bytes 262144 | tf_op jit(solution)/shard_map/all_to_all | solution.py:309
  74.0 8.7 %all_to_all.27.pieces_ref = bf16[4,32,512]{2,1,0:T(8,128)(2,1)S(1)} all-to-all(bf16[4,32,512]{2,1,0:T(8,128)(2,1)S(1)} %add_shares.1), channel_id=1, replica_groups={{256,128,384,0},{288,160,416,32},{320,192,448,64},{352,224,480,96},{112..., dimensions={0} | all-to-all | bytes 262144 | tf_op jit(solution)/shard_map/all_to_all | solution.py:309
  82.7 0.0 copy-done.8
  82.7 0.0 copy-done.10
  82.7 0.0 copy-start.2
  82.7 0.0 copy-start.4
  82.7 0.5 project.1
  83.2 11.6 %all_to_all.28.rows_ref = bf16[16,32,512]{2,1,0:T(8,128)(2,1)S(1)} all-to-all(bf16[16,32,512]{2,1,0:T(8,128)(2,1)S(1)} %project.1), channel_id=1, replica_groups={{15,14,13,12,11,10,9,8,7,6,5,4,3,2,1,0},{31,30,29,28,27,26,25,24,23,22,..., dimensions={0} | all-to-all | bytes 1048576 | tf_op jit(solution)/shard_map/all_to_all | solution.py:309
  94.9 6.8 %collective-permute-start.1 = (bf16[16,32,512]{2,1,0:T(8,128)(2,1)S(1)}, bf16[16,32,512]{2,1,0:T(8,128)(2,1)S(1)}, u32[]{:S(2)}, u32[]{:S(2)}) collective-permute-start(bf16[16,32,512]{2,1,0:T(8,128)(2,1)S(1)} %all_to_all.28.rows_ref), channel_id=1, source_target_pairs={{0,16},{16,0},{32,48},{48,32},{64,80},{80,64},{96,112},{112,96},{1... | collective-permute-start | bytes 1572872 | tf_op jit(solution)/shard_map/ppermute | solution.py:369
  101.7 1.0 unpack.1
  102.6 0.0 copy-done.2
  102.6 0.0 copy-done.4
  102.6 1.2 %finish_own.1.first_ref = f32[2,512,512]{2,1,0:T(8,128)S(1)} custom-call(bf16[16,32,512]{2,1,0:T(8,128)(2,1)S(1)} %all_to_all.28.rows_ref, bf16[2,1024,512]{2,1,0:T(8,128)(2,1)S(1)} %copy-done.2, bf16[2,1024,512]{2,1,0:T(8,128)(2,1)S(1)} %copy-done.4), custom_call_target="tpu_custom_call" | custom-call | flops 1000000000 | bytes 6815744 | tf_op jit(solution)/shard_map/finish_own/pallas_call | solution.py:296
  103.9 0.0 collective-permute-done.1.rows_ref
  103.9 2.1 %finish_other.1 = f32[2,512,512]{2,1,0:T(8,128)} custom-call(bf16[16,32,512]{2,1,0:T(8,128)(2,1)S(1)} %collective-permute-done.1.rows_ref, bf16[2,1024,512]{2,1,0:T(8,128)(2,1)S(1)} %copy-done.2, bf16[2,1024,512]{2,1,0:T(8,128)(2,1)S(1)} %copy-done.4, f32[2,512,512]{2,1,0:T(8,128)S(1)} %finish_own.1.first_ref), custom_call_target="tpu_custom_call" | custom-call | flops 1000000000 | bytes 8912896 | tf_op jit(solution)/shard_map/finish_other/pallas_call | solution.py:296
  (1 shorter events, 0.0 us)
Async XLA Ops:
  0.6 11.7 %copy-start = (f32[2,512,512]{2,1,0:T(8,128)S(1)}, f32[2,512,512]{2,1,0:T(8,128)}, u32[]{:S(2)}) copy-start(f32[2,512,512]{2,1,0:T(8,128)} %ritz_ref.2) | copy-start | bytes 6291460
  3.0 21.3 %all-to-all-start = ((bf16[16,288,128]{2,1,0:T(8,128)(2,1)}), bf16[16,288,128]{2,1,0:T(8,128)(2,1)S(1)}, u32[]{:S(2)}, u32[]{:S(2)}) async-start(bf16[16,288,128]{2,1,0:T(8,128)(2,1)} %pack.1), calls=%async_computation | async-start | bytes 2359296 | tf_op jit(solution)/shard_map/all_to_all | solution.py:309
  12.8 1.3 %copy-start.5 = (bf16[1024,1024]{1,0:T(8,128)(2,1)}, bf16[1024,1024]{1,0:T(8,128)(2,1)S(1)}, u32[]{:S(2)}) copy-start(bf16[1024,1024]{1,0:T(8,128)(2,1)S(1)} %turn_matrix.1.turn_ref) | copy-start | bytes 6291460
  14.4 1.0 copy-start.7
  15.4 1.0 copy-start.9
  17.5 1.3 %copy-start.1 = (bf16[2,1024,512]{2,1,0:T(8,128)(2,1)}, bf16[2,1024,512]{2,1,0:T(8,128)(2,1)S(1)}, u32[]{:S(2)}) copy-start(bf16[2,1024,512]{2,1,0:T(8,128)(2,1)S(1)} %get-tuple-element.28.high_ref) | copy-start | bytes 6291460
  18.9 1.3 %copy-start.3 = (bf16[2,1024,512]{2,1,0:T(8,128)(2,1)}, bf16[2,1024,512]{2,1,0:T(8,128)(2,1)S(1)}, u32[]{:S(2)}) copy-start(bf16[2,1024,512]{2,1,0:T(8,128)(2,1)S(1)} %get-tuple-element.29.low_ref) | copy-start | bytes 6291460
  25.1 7.0 %copy-start.6 = (bf16[1024,1024]{1,0:T(8,128)(2,1)S(1)}, bf16[1024,1024]{1,0:T(8,128)(2,1)}, u32[]{:S(2)}) copy-start(bf16[1024,1024]{1,0:T(8,128)(2,1)} %copy-done.5) | copy-start | bytes 6291460
  25.1 8.4 %collective-permute-start = (bf16[16,128,128]{2,1,0:T(8,128)(2,1)S(1)}, bf16[16,128,128]{2,1,0:T(8,128)(2,1)S(1)}, u32[]{:S(2)}, u32[]{:S(2)}) collective-permute-start(bf16[16,128,128]{2,1,0:T(8,128)(2,1)S(1)} %share_given.1), channel_id=1, source_target_pairs={{0,16},{16,0},{32,48},{48,32},{64,80},{80,64},{96,112},{112,96},{1... | collective-permute-start | bytes 1572872 | tf_op jit(solution)/shard_map/ppermute | solution.py:349
  33.6 49.1 %copy-start.8 = (bf16[2,512,512]{2,1,0:T(8,128)(2,1)S(1)}, bf16[2,512,512]{2,1,0:T(8,128)(2,1)}, u32[]{:S(2)}) copy-start(bf16[2,512,512]{2,1,0:T(8,128)(2,1)} %copy-done.7) | copy-start | bytes 3145732
  33.6 49.1 %copy-start.10 = (bf16[2,512,512]{2,1,0:T(8,128)(2,1)S(1)}, bf16[2,512,512]{2,1,0:T(8,128)(2,1)}, u32[]{:S(2)}) copy-start(bf16[2,512,512]{2,1,0:T(8,128)(2,1)} %copy-done.9) | copy-start | bytes 3145732
  82.7 19.9 %copy-start.2 = (bf16[2,1024,512]{2,1,0:T(8,128)(2,1)S(1)}, bf16[2,1024,512]{2,1,0:T(8,128)(2,1)}, u32[]{:S(2)}) copy-start(bf16[2,1024,512]{2,1,0:T(8,128)(2,1)} %copy-done.1) | copy-start | bytes 6291460
  82.7 19.9 %copy-start.4 = (bf16[2,1024,512]{2,1,0:T(8,128)(2,1)S(1)}, bf16[2,1024,512]{2,1,0:T(8,128)(2,1)}, u32[]{:S(2)}) copy-start(bf16[2,1024,512]{2,1,0:T(8,128)(2,1)} %copy-done.3) | copy-start | bytes 6291460
  94.9 9.0 %collective-permute-start.1 = (bf16[16,32,512]{2,1,0:T(8,128)(2,1)S(1)}, bf16[16,32,512]{2,1,0:T(8,128)(2,1)S(1)}, u32[]{:S(2)}, u32[]{:S(2)}) collective-permute-start(bf16[16,32,512]{2,1,0:T(8,128)(2,1)S(1)} %all_to_all.28.rows_ref), channel_id=1, source_target_pairs={{0,16},{16,0},{32,48},{48,32},{64,80},{80,64},{96,112},{112,96},{1... | collective-permute-start | bytes 1572872 | tf_op jit(solution)/shard_map/ppermute | solution.py:369

commit v5 on v4

--- a/solution.py
+++ b/solution.py
@@ -24,7 +24,7 @@
 PIECE_ROWS = TAIL_ROW + HALF
 DEPTH = 2 * MAIN + LANES
 SHARE_ROWS = 8 * HALF
-CHUNKS = 2
+CHUNKS = 4
 NEAR = 4
 
 REVERSED = list(range(PEERS))[::-1]
@@ -41,61 +41,58 @@
     return pltpu.roll(values, shift, len(values.shape) - 1) if shift else values
 
 
-def pack_kernel(vectors_hbm, images_hbm, out_hbm, vectors_ref, images_ref, out_ref, arrived, sent):
+def pack_kernel(vectors_hbm, images_hbm, out_hbm, sources_ref, out_ref, arrived, sent):
     peers = PEERS // CHUNKS
-    copies = []
-    for which, (source, target) in enumerate(((vectors_hbm, vectors_ref), (images_hbm, images_ref))):
-        for chunk in range(CHUNKS + 1):
-            at = chunk * peers * MAIN
-            lanes = pl.ds(at, TAIL_AT // CHUNKS if chunk < CHUNKS else 4 * LANES)
-            copy = pltpu.make_async_copy(
-                source.at[:, :, lanes], target.at[:, :, lanes], arrived.at[which * (CHUNKS + 1) + chunk]
+    copies, leaving = {}, []
+    for chunk in (CHUNKS, *range(CHUNKS)):
+        for which, source in enumerate((vectors_hbm, images_hbm)):
+            lanes = pl.ds(chunk * peers * MAIN, peers * MAIN if chunk < CHUNKS else 4 * LANES)
+            copies[which, chunk] = pltpu.make_async_copy(
+                source.at[:, :, lanes], sources_ref.at[which, :, :, lanes], arrived.at[which * (CHUNKS + 1) + chunk]
             )
-            copy.start()
-            copies.append(copy)
+            copies[which, chunk].start()
     group = lane_group((HALF, LANES))
-    leaving = []
-    for which, source_ref in enumerate((vectors_ref, images_ref)):
-        base = which * PIECE_ROWS
-        for chunk in range(CHUNKS + 1):
-            index = which * (CHUNKS + 1) + chunk
-            copies[index].wait()
-            if chunk < CHUNKS:
-                for peer in range(chunk * peers, (chunk + 1) * peers):
-                    for block in range(2):
-                        at = peer * MAIN + block * LANES
-                        for part in range(2):
-                            row = base + (block * 2 + part) * OWNED
-                            out_ref[REVERSED[peer], row : row + OWNED, :] = source_ref[part, :, at : at + LANES]
-                where = (pl.ds(PEERS - (chunk + 1) * peers, peers), pl.ds(base, TAIL_ROW))
-            else:
-                for block in range(PEERS // 4):
-                    at = TAIL_AT + block * LANES
-                    tails = [
-                        source_ref[part, half * HALF : (half + 1) * HALF, at : at + LANES].astype(F32)
-                        for part in range(2)
-                        for half in range(2)
+    for which in range(2):
+        copies[which, CHUNKS].wait()
+        for block in range(PEERS // 4):
+            at = slice(TAIL_AT + block * LANES, TAIL_AT + (block + 1) * LANES)
+            tails = [
+                sources_ref[which, part, half * HALF : (half + 1) * HALF, at].astype(F32)
+                for part in range(2)
+                for half in range(2)
+            ]
+            for quarter in range(4):
+                packed = turn(tails[0], -quarter)
+                for slot in range(1, 4):
+                    packed = jnp.where(group == slot, turn(tails[slot], slot - quarter), packed)
+                place, lanes = REVERSED[block * 4 + quarter], slice(which * LANES, (which + 1) * LANES)
+                out_ref[place, 4 * OWNED : 4 * OWNED + HALF, lanes] = packed.astype(BF16)
+    for chunk in range(CHUNKS):
+        for which in range(2):
+            copies[which, chunk].wait()
+            for peer in range(chunk * peers, (chunk + 1) * peers):
+                for part in range(2):
+                    row = (which * 2 + part) * OWNED
+                    out_ref[REVERSED[peer], row : row + OWNED, :] = sources_ref[
+                        which, part, :, peer * MAIN : (peer + 1) * MAIN
                     ]
-                    for quarter in range(4):
-                        packed = turn(tails[0], -quarter)
-                        for slot in range(1, 4):
-                            packed = jnp.where(group == slot, turn(tails[slot], slot - quarter), packed)
-                        out_ref[REVERSED[block * 4 + quarter], base + TAIL_ROW : base + PIECE_ROWS, :] = packed.astype(BF16)
-                where = (pl.ds(0, PEERS), pl.ds(base + TAIL_ROW, HALF))
-            copy = pltpu.make_async_copy(out_ref.at[where], out_hbm.at[where], sent.at[index])
-            copy.start()
-            leaving.append(copy)
+        places = pl.ds(PEERS - (chunk + 1) * peers, peers)
+        copy = pltpu.make_async_copy(out_ref.at[places], out_hbm.at[places], sent.at[chunk])
+        copy.start()
+        leaving.append(copy)
     for copy in leaving:
         copy.wait()
 
 
-def of_owners(got_ref, rows):
-    return jnp.concatenate([got_ref[at, rows, :] for at in REVERSED], axis=0)
-
-
-def tails_of(got_ref, base):
-    values = of_owners(got_ref, slice(base + TAIL_ROW, base + PIECE_ROWS)).astype(F32)
-    return values.reshape(PEERS, HALF, LANES)
+def main_of(got_ref, which, part):
+    at = (which * 2 + part) * OWNED
+    return jnp.concatenate([got_ref[place, at : at + OWNED, :] for place in REVERSED], axis=0)
+
+
+def tails_of(got_ref, which, places):
+    lanes = slice(which * LANES, (which + 1) * LANES)
+    values = [got_ref[place, 4 * OWNED : 4 * OWNED + HALF, lanes] for place in places]
+    return jnp.concatenate(values, axis=0).astype(F32).reshape(PEERS, HALF, LANES)
 
 
 def unpack_kernel(back_ref, out_ref):
@@ -145,12 +142,10 @@
 
 
 def rotate_kernel(got_ref, turn_ref, out_ref, stacked):
-    packed = tails_of(got_ref, 0)
+    packed = tails_of(got_ref, 0, REVERSED)
     for part in range(2):
         rows = slice(part * MODES, (part + 1) * MODES)
-        for block in range(2):
-            at = (block * 2 + part) * OWNED
-            stacked[rows, block * LANES : (block + 1) * LANES] = of_owners(got_ref, slice(at, at + OWNED))
+        stacked[rows, 0:MAIN] = main_of(got_ref, 0, part)
         ends = jnp.concatenate([turn(packed, -2 * part), turn(packed, -2 * part - 1)], axis=1)
         stacked[rows, MAIN : MAIN + LANES] = ends.reshape(MODES, LANES).astype(BF16)
 
@@ -184,24 +179,19 @@
         first, second = (turn(packed, place - 2 * sources[place] - row_half) * signs[place] for place in range(2))
         return jnp.where(group == 0, first, jnp.where(group == 1, second, 0.0))
 
-    packed = got_ref[:, TAIL_ROW:PIECE_ROWS, :].astype(F32)
-    for part in range(2):
-        for block in range(2):
-            row = pl.multiple_of((block * 2 + part) * OWNED + half * HALF, HALF)
-            at = part * MAIN + block * LANES
-            left[:, at : at + LANES] = got_ref[:, pl.ds(row, HALF), :].reshape(HALF_MODES, LANES)
+    packed = tails_of(got_ref, 0, range(PEERS))
+    for part in range(2):
+        row = pl.multiple_of(part * OWNED + half * HALF, HALF)
+        left[:, part * MAIN : (part + 1) * MAIN] = got_ref[:, pl.ds(row, HALF), :].reshape(HALF_MODES, MAIN)
     ends = jnp.where(half == 0, side(packed, 0, (0, 1), (1, 1)), side(packed, 1, (0, 1), (1, 1)))
     left[:, 2 * MAIN : DEPTH] = ends.reshape(HALF_MODES, LANES).astype(BF16)
 
-    packed = tails_of(got_ref, PIECE_ROWS)
+    packed = tails_of(got_ref, 1, REVERSED)
     for part in range(2):
         sources, signs = ((0, 1), (1, 1)) if part == 0 else ((1, 0), (1, -1))
         for place in range(2):
-            for block in range(2):
-                at = PIECE_ROWS + (block * 2 + sources[place]) * OWNED
-                values = of_owners(got_ref, slice(at, at + OWNED))
-                lanes = slice(place * MAIN + block * LANES, place * MAIN + (block + 1) * LANES)
-                right[part, :, lanes] = values if signs[place] > 0 else -values
+            values = main_of(got_ref, 1, sources[place])
+            right[part, :, place * MAIN : (place + 1) * MAIN] = values if signs[place] > 0 else -values
         ends = jnp.concatenate([side(packed, row_half, sources, signs) for row_half in range(2)], axis=1)
         right[part, :, 2 * MAIN : DEPTH] = ends.reshape(MODES, LANES).astype(BF16)
     for part in range(2):
@@ -322,15 +312,14 @@
     packed = call(
         pack_kernel,
         "pack",
-        [((PEERS, 2 * PIECE_ROWS, LANES), BF16)],
+        [((PEERS, 4 * OWNED + HALF, MAIN), BF16)],
         vectors,
         images,
         scratch=[
-            pltpu.VMEM((2, OWNED, width), BF16),
-            pltpu.VMEM((2, OWNED, width), BF16),
-            pltpu.VMEM((PEERS, 2 * PIECE_ROWS, LANES), BF16),
+            pltpu.VMEM((2, 2, OWNED, width), BF16),
+            pltpu.VMEM((PEERS, 4 * OWNED + HALF, MAIN), BF16),
             pltpu.SemaphoreType.DMA((2 * CHUNKS + 2,)),
-            pltpu.SemaphoreType.DMA((2 * CHUNKS + 2,)),
+            pltpu.SemaphoreType.DMA((CHUNKS,)),
         ],
         in_place=True,
         out_place=True,
@@ -360,9 +349,9 @@
     sent = call(assemble_kernel, "assemble", [((PEERS, SHARE_ROWS + PIECE_ROWS, LANES), BF16)], kept, taken, turned)
     back = exchange(sent, "mode", [REVERSED])
     summed = call(sum_kernel, "sum_shares", [((NEAR, OWNED, MODES), BF16)], back)
+    summed = exchange(summed, "site", far_groups[0] + near_groups[1])
+    summed = call(add_kernel, "add_shares", [((NEAR, OWNED, MODES), BF16)], summed)
     summed = exchange(summed, "site", near_groups[0] + far_groups[1])
-    summed = call(add_kernel, "add_shares", [((NEAR, OWNED, MODES), BF16)], summed)
-    summed = exchange(summed, "site", far_groups[0] + near_groups[1])
     rows = call(project_kernel, "project", [((PEERS, OWNED, MODES), BF16)], summed, *ritz_split)
     own = exchange(rows, "mode", [REVERSED])
     own, back = lax.optimization_barrier((own, back))

time: 107 us -> 106 us (level)
  starting transfers between devices: 22.4 us -> 23.6 us
    ppermute x1, starting transfers between devices: 6.79 us -> 8 us  [on_device(): other = lax.ppermute(own, 'site', swap)]
where the time goes in v5:
time: 106 us
  blocking collectives  59.6 us (56%)
  starting transfers between devices  23.6 us (22%)
  Pallas kernels  12 us (11%)
  local copies, waits for them, and re-layouts  5.94 us (6%)
  waiting for transfers between devices  4.12 us (4%)
    all_to_all x4, blocking collectives, exchange(): return lax.all_to_all(pieces, axis, 0, 0, axis_index_groups=groups)  59.6 us
    pallas_call x14, Pallas kernels, call(): pl.pallas_call(kernel, name=name, out_shape=outs[0] if single else outs,...  12 us
    all_to_all x1, starting transfers between devices, exchange(): return lax.all_to_all(pieces, axis, 0, 0, axis_index_groups=groups)  9.35 us
    ppermute x1, starting transfers between devices, on_device(): other = lax.ppermute(own, 'site', swap)  8 us
    ppermute x1, starting transfers between devices, on_device(): taken = lax.ppermute(given, 'site', swap)  6.2 us
    unnamed x22, local copies, waits for them, and re-layouts  5.94 us
    all_to_all x1, waiting for transfers between devices, exchange(): return lax.all_to_all(pieces, axis, 0, 0, axis_index_groups=groups)  4.11 us
  transfers between devices with their start and end apart: 3, of which 1 were waited for; matrix products, arithmetic and copies ran while one was open for 0% of the time, Pallas kernels for 6%

profile of v5, /device:TPU:1, one launch (start us, length us, event | category | flops | bytes accessed | tf_op | source)
XLA Modules:
  0.0 106.0 jit_solution(8770500685924316381)
XLA Ops:
  0.6 0.0 copy-start
  0.6 2.4 %pack.1 = bf16[16,144,256]{2,1,0:T(8,128)(2,1)} custom-call(bf16[2,32,4608]{2,1,0:T(8,128)(2,1)} %vectors_hbm.1, bf16[2,32,4608]{2,1,0:T(8,128)(2,1)} %images_hbm.1), custom_call_target="tpu_custom_call" | custom-call | bytes 2359296 | tf_op jit(solution)/shard_map/pack/pallas_call | solution.py:286
  3.0 9.4 %all-to-all-start = ((bf16[16,144,256]{2,1,0:T(8,128)(2,1)}), bf16[16,144,256]{2,1,0:T(8,128)(2,1)S(1)}, u32[]{:S(2)}, u32[]{:S(2)}) async-start(bf16[16,144,256]{2,1,0:T(8,128)(2,1)} %pack.1), calls=%async_computation | async-start | bytes 2359296 | tf_op jit(solution)/shard_map/all_to_all | solution.py:299
  12.4 0.0 copy-done
  12.4 0.5 turn_matrix.1.turn_ref
  12.9 0.0 copy-start.5
  12.9 1.3 %copy-done.5 = bf16[1024,1024]{1,0:T(8,128)(2,1)} copy-done((bf16[1024,1024]{1,0:T(8,128)(2,1)}, bf16[1024,1024]{1,0:T(8,128)(2,1)S(1)}, u32[]{:S(2)}) %copy-start.5) | copy-done | bytes 2097176
  14.2 0.3 split_ritz.1
  14.5 0.0 copy-start.7
  14.5 1.0 copy-done.7
  15.5 0.0 copy-start.9
  15.5 1.0 copy-done.9
  16.4 1.1 %left_factors.1 = (bf16[2,1024,512]{2,1,0:T(8,128)(2,1)S(1)}, bf16[2,1024,512]{2,1,0:T(8,128)(2,1)S(1)}) custom-call(f32[2,512,512]{2,1,0:T(8,128)S(1)} %copy-done), custom_call_target="tpu_custom_call" | custom-call | bytes 6291456 | tf_op jit(solution)/shard_map/left_factors/pallas_call | solution.py:286
  17.6 0.0 copy-start.1
  17.6 1.3 %copy-done.1 = bf16[2,1024,512]{2,1,0:T(8,128)(2,1)} copy-done((bf16[2,1024,512]{2,1,0:T(8,128)(2,1)}, bf16[2,1024,512]{2,1,0:T(8,128)(2,1)S(1)}, u32[]{:S(2)}) %copy-start.1) | copy-done | bytes 2097176
  18.9 0.0 copy-start.3
  18.9 1.3 %copy-done.3 = bf16[2,1024,512]{2,1,0:T(8,128)(2,1)} copy-done((bf16[2,1024,512]{2,1,0:T(8,128)(2,1)}, bf16[2,1024,512]{2,1,0:T(8,128)(2,1)S(1)}, u32[]{:S(2)}) %copy-start.3) | copy-done | bytes 2097176
  20.3 4.1 %all-to-all-done.got_ref = bf16[16,144,256]{2,1,0:T(8,128)(2,1)S(1)} async-done(((bf16[16,144,256]{2,1,0:T(8,128)(2,1)}), bf16[16,144,256]{2,1,0:T(8,128)(2,1)S(1)}, u32[]{:S(2)}, u32[]{:S(2)}) %all-to-all-start) | async-done | bytes 1179680 | tf_op jit(solution)/shard_map/all_to_all | solution.py:299
  24.4 0.6 share_given.1
  25.0 0.0 copy-start.6
  25.0 6.2 %collective-permute-start = (bf16[16,128,128]{2,1,0:T(8,128)(2,1)S(1)}, bf16[16,128,128]{2,1,0:T(8,128)(2,1)S(1)}, u32[]{:S(2)}, u32[]{:S(2)}) collective-permute-start(bf16[16,128,128]{2,1,0:T(8,128)(2,1)S(1)} %share_given.1), channel_id=1, source_target_pairs={{0,16},{16,0},{32,48},{48,32},{64,80},{80,64},{96,112},{112,96},{1... | collective-permute-start | bytes 1572872 | tf_op jit(solution)/shard_map/ppermute | solution.py:338
  31.2 0.6 share_kept.1.kept_ref
  31.9 0.0 copy-done.6
  31.9 1.4 %rotate.1.turned_ref = bf16[16,144,128]{2,1,0:T(8,128)(2,1)S(1)} custom-call(bf16[16,144,256]{2,1,0:T(8,128)(2,1)S(1)} %all-to-all-done.got_ref, bf16[1024,1024]{1,0:T(8,128)(2,1)S(1)} %copy-done.6), custom_call_target="tpu_custom_call" | custom-call | flops 1000000000 | bytes 3866624 | tf_op jit(solution)/shard_map/rotate/pallas_call | solution.py:286
  33.3 0.0 collective-permute-done.taken_ref
  33.3 0.1 assemble.1
  33.4 0.0 copy-start.8
  33.4 0.0 copy-start.10
  33.4 21.1 %all_to_all.25.back_ref = bf16[16,272,128]{2,1,0:T(8,128)(2,1)S(1)} all-to-all(bf16[16,272,128]{2,1,0:T(8,128)(2,1)S(1)} %assemble.1), channel_id=1, replica_groups={{15,14,13,12,11,10,9,8,7,6,5,4,3,2,1,0},{31,30,29,28,27,26,25,24,23,22,..., dimensions={0} | all-to-all | bytes 2228224 | tf_op jit(solution)/shard_map/all_to_all | solution.py:299
  54.5 0.1 sum_shares.1
  54.6 9.7 %all_to_all.26.pieces_ref = bf16[4,32,512]{2,1,0:T(8,128)(2,1)S(1)} all-to-all(bf16[4,32,512]{2,1,0:T(8,128)(2,1)S(1)} %sum_shares.1), channel_id=1, replica_groups={{256,128,384,0},{288,160,416,32},{320,192,448,64},{352,224,480,96},{112..., dimensions={0} | all-to-all | bytes 262144 | tf_op jit(solution)/shard_map/all_to_all | solution.py:299
  64.3 17.2 %all_to_all.27.pieces_ref = bf16[4,32,512]{2,1,0:T(8,128)(2,1)S(1)} all-to-all(bf16[4,32,512]{2,1,0:T(8,128)(2,1)S(1)} %add_shares.1), channel_id=1, replica_groups={{96,64,32,0},{224,192,160,128},{352,320,288,256},{480,448,416,384},{272..., dimensions={0} | all-to-all | bytes 262144 | tf_op jit(solution)/shard_map/all_to_all | solution.py:299
  81.5 0.0 copy-done.8
  81.5 0.0 copy-done.10
  81.5 0.0 copy-start.2
  81.5 0.0 copy-start.4
  81.5 0.5 project.1
  82.0 11.6 %all_to_all.28.rows_ref = bf16[16,32,512]{2,1,0:T(8,128)(2,1)S(1)} all-to-all(bf16[16,32,512]{2,1,0:T(8,128)(2,1)S(1)} %project.1), channel_id=1, replica_groups={{15,14,13,12,11,10,9,8,7,6,5,4,3,2,1,0},{31,30,29,28,27,26,25,24,23,22,..., dimensions={0} | all-to-all | bytes 1048576 | tf_op jit(solution)/shard_map/all_to_all | solution.py:299
  93.6 8.0 %collective-permute-start.1 = (bf16[16,32,512]{2,1,0:T(8,128)(2,1)S(1)}, bf16[16,32,512]{2,1,0:T(8,128)(2,1)S(1)}, u32[]{:S(2)}, u32[]{:S(2)}) collective-permute-start(bf16[16,32,512]{2,1,0:T(8,128)(2,1)S(1)} %all_to_all.28.rows_ref), channel_id=1, source_target_pairs={{0,16},{16,0},{32,48},{48,32},{64,80},{80,64},{96,112},{112,96},{1... | collective-permute-start | bytes 1572872 | tf_op jit(solution)/shard_map/ppermute | solution.py:358
  101.7 1.0 unpack.1
  102.6 0.0 copy-done.2
  102.6 0.0 copy-done.4
  102.6 1.2 %finish_own.1.first_ref = f32[2,512,512]{2,1,0:T(8,128)S(1)} custom-call(bf16[16,32,512]{2,1,0:T(8,128)(2,1)S(1)} %all_to_all.28.rows_ref, bf16[2,1024,512]{2,1,0:T(8,128)(2,1)S(1)} %copy-done.2, bf16[2,1024,512]{2,1,0:T(8,128)(2,1)S(1)} %copy-done.4), custom_call_target="tpu_custom_call" | custom-call | flops 1000000000 | bytes 6815744 | tf_op jit(solution)/shard_map/finish_own/pallas_call | solution.py:286
  103.9 0.0 collective-permute-done.1.rows_ref
  103.9 2.1 %finish_other.1 = f32[2,512,512]{2,1,0:T(8,128)} custom-call(bf16[16,32,512]{2,1,0:T(8,128)(2,1)S(1)} %collective-permute-done.1.rows_ref, bf16[2,1024,512]{2,1,0:T(8,128)(2,1)S(1)} %copy-done.2, bf16[2,1024,512]{2,1,0:T(8,128)(2,1)S(1)} %copy-done.4, f32[2,512,512]{2,1,0:T(8,128)S(1)} %finish_own.1.first_ref), custom_call_target="tpu_custom_call" | custom-call | flops 1000000000 | bytes 8912896 | tf_op jit(solution)/shard_map/finish_other/pallas_call | solution.py:286
  (1 shorter events, 0.0 us)
Async XLA Ops:
  0.6 11.8 %copy-start = (f32[2,512,512]{2,1,0:T(8,128)S(1)}, f32[2,512,512]{2,1,0:T(8,128)}, u32[]{:S(2)}) copy-start(f32[2,512,512]{2,1,0:T(8,128)} %ritz_ref.2) | copy-start | bytes 6291460
  3.0 21.3 %all-to-all-start = ((bf16[16,144,256]{2,1,0:T(8,128)(2,1)}), bf16[16,144,256]{2,1,0:T(8,128)(2,1)S(1)}, u32[]{:S(2)}, u32[]{:S(2)}) async-start(bf16[16,144,256]{2,1,0:T(8,128)(2,1)} %pack.1), calls=%async_computation | async-start | bytes 2359296 | tf_op jit(solution)/shard_map/all_to_all | solution.py:299
  12.9 1.3 %copy-start.5 = (bf16[1024,1024]{1,0:T(8,128)(2,1)}, bf16[1024,1024]{1,0:T(8,128)(2,1)S(1)}, u32[]{:S(2)}) copy-start(bf16[1024,1024]{1,0:T(8,128)(2,1)S(1)} %turn_matrix.1.turn_ref) | copy-start | bytes 6291460
  14.5 1.0 copy-start.7
  15.5 1.0 copy-start.9
  17.6 1.3 %copy-start.1 = (bf16[2,1024,512]{2,1,0:T(8,128)(2,1)}, bf16[2,1024,512]{2,1,0:T(8,128)(2,1)S(1)}, u32[]{:S(2)}) copy-start(bf16[2,1024,512]{2,1,0:T(8,128)(2,1)S(1)} %get-tuple-element.28.high_ref) | copy-start | bytes 6291460
  18.9 1.3 %copy-start.3 = (bf16[2,1024,512]{2,1,0:T(8,128)(2,1)}, bf16[2,1024,512]{2,1,0:T(8,128)(2,1)S(1)}, u32[]{:S(2)}) copy-start(bf16[2,1024,512]{2,1,0:T(8,128)(2,1)S(1)} %get-tuple-element.29.low_ref) | copy-start | bytes 6291460
  25.0 6.9 %copy-start.6 = (bf16[1024,1024]{1,0:T(8,128)(2,1)S(1)}, bf16[1024,1024]{1,0:T(8,128)(2,1)}, u32[]{:S(2)}) copy-start(bf16[1024,1024]{1,0:T(8,128)(2,1)} %copy-done.5) | copy-start | bytes 6291460
  25.0 8.3 %collective-permute-start = (bf16[16,128,128]{2,1,0:T(8,128)(2,1)S(1)}, bf16[16,128,128]{2,1,0:T(8,128)(2,1)S(1)}, u32[]{:S(2)}, u32[]{:S(2)}) collective-permute-start(bf16[16,128,128]{2,1,0:T(8,128)(2,1)S(1)} %share_given.1), channel_id=1, source_target_pairs={{0,16},{16,0},{32,48},{48,32},{64,80},{80,64},{96,112},{112,96},{1... | collective-permute-start | bytes 1572872 | tf_op jit(solution)/shard_map/ppermute | solution.py:338
  33.4 48.1 %copy-start.8 = (bf16[2,512,512]{2,1,0:T(8,128)(2,1)S(1)}, bf16[2,512,512]{2,1,0:T(8,128)(2,1)}, u32[]{:S(2)}) copy-start(bf16[2,512,512]{2,1,0:T(8,128)(2,1)} %copy-done.7) | copy-start | bytes 3145732
  33.4 48.1 %copy-start.10 = (bf16[2,512,512]{2,1,0:T(8,128)(2,1)S(1)}, bf16[2,512,512]{2,1,0:T(8,128)(2,1)}, u32[]{:S(2)}) copy-start(bf16[2,512,512]{2,1,0:T(8,128)(2,1)} %copy-done.9) | copy-start | bytes 3145732
  81.5 21.1 %copy-start.2 = (bf16[2,1024,512]{2,1,0:T(8,128)(2,1)S(1)}, bf16[2,1024,512]{2,1,0:T(8,128)(2,1)}, u32[]{:S(2)}) copy-start(bf16[2,1024,512]{2,1,0:T(8,128)(2,1)} %copy-done.1) | copy-start | bytes 6291460
  81.5 21.1 %copy-start.4 = (bf16[2,1024,512]{2,1,0:T(8,128)(2,1)S(1)}, bf16[2,1024,512]{2,1,0:T(8,128)(2,1)}, u32[]{:S(2)}) copy-start(bf16[2,1024,512]{2,1,0:T(8,128)(2,1)} %copy-done.3) | copy-start | bytes 6291460
  93.6 10.2 %collective-permute-start.1 = (bf16[16,32,512]{2,1,0:T(8,128)(2,1)S(1)}, bf16[16,32,512]{2,1,0:T(8,128)(2,1)S(1)}, u32[]{:S(2)}, u32[]{:S(2)}) collective-permute-start(bf16[16,32,512]{2,1,0:T(8,128)(2,1)S(1)} %all_to_all.28.rows_ref), channel_id=1, source_target_pairs={{0,16},{16,0},{32,48},{48,32},{64,80},{80,64},{96,112},{112,96},{1... | collective-permute-start | bytes 1572872 | tf_op jit(solution)/shard_map/ppermute | solution.py:358

commit v6 on v5

--- a/solution.py
+++ b/solution.py
@@ -261,7 +261,7 @@
         out_ref[part] = finish_products(core, rows_ref, high_ref, low_ref, pl.ds(part * MODES, MODES))
 
 
-def finish_other_kernel(rows_ref, high_ref, low_ref, first_ref, out_hbm, total, sent):
+def finish_other_kernel(rows_ref, high_ref, low_ref, first_ref, back_ref, out_hbm, rotated_hbm, total, rotated, sent):
     core = lax.rem(lax.axis_index("site"), 2)
     copies = []
     for part in range(2):
@@ -272,8 +272,11 @@
             copy = pltpu.make_async_copy(total.at[part, rows, :], out_hbm.at[part, rows, :], sent.at[part * 2 + half])
             copy.start()
             copies.append(copy)
-    for copy in copies:
-        copy.wait()
+    unpack_kernel(back_ref, rotated)
+    copy = pltpu.make_async_copy(rotated, rotated_hbm, sent.at[4])
+    copy.start()
+    for done in copies + [copy]:
+        done.wait()
 
 
 def call(kernel, name, outs, *args, flops=0, scratch=(), in_place=False, out_place=False, vmem=16):
@@ -354,20 +357,19 @@
     summed = exchange(summed, "site", near_groups[0] + far_groups[1])
     rows = call(project_kernel, "project", [((PEERS, OWNED, MODES), BF16)], summed, *ritz_split)
     own = exchange(rows, "mode", [REVERSED])
-    own, back = lax.optimization_barrier((own, back))
     other = lax.ppermute(own, "site", swap)
-    rotated = call(unpack_kernel, "unpack", local, back)
     whole = [((2, MODES, MODES), F32)]
     first = call(finish_own_kernel, "finish_own", whole, own, *left, flops=10**9)
-    projected = call(
+    projected, rotated = call(
         finish_other_kernel,
         "finish_other",
-        whole,
+        whole + local,
         other,
         *left,
         first,
+        back,
         flops=10**9,
-        scratch=[pltpu.VMEM((2, MODES, MODES), F32), pltpu.SemaphoreType.DMA((4,))],
+        scratch=[pltpu.VMEM((2, MODES, MODES), F32), pltpu.VMEM(*local[0]), pltpu.SemaphoreType.DMA((5,))],
         out_place=True,
     )
     return rotated, projected

time: 106 us -> 106 us (level)
    pallas_call x14 -> x13, Pallas kernels: 12 us -> 11.3 us  [call(): pl.pallas_call(kernel, name=name, out_shape=outs[0] if single else outs,...]
  transfers between devices with their start and end apart: 3 -> 3, of which waited for: 1 -> 2; matrix products, arithmetic and copies ran while one was open for 0% -> 0% of each run, Pallas kernels for 6% -> 5%
where the time goes in v6:
time: 106 us
  blocking collectives  59.7 us (56%)
  starting transfers between devices  23.5 us (22%)
  Pallas kernels  11.3 us (11%)
  local copies, waits for them, and re-layouts  5.95 us (6%)
  waiting for transfers between devices  4.34 us (4%)
    all_to_all x4, blocking collectives, exchange(): return lax.all_to_all(pieces, axis, 0, 0, axis_index_groups=groups)  59.7 us
    pallas_call x13, Pallas kernels, call(): pl.pallas_call(kernel, name=name, out_shape=outs[0] if single else outs,...  11.3 us
    all_to_all x1, starting transfers between devices, exchange(): return lax.all_to_all(pieces, axis, 0, 0, axis_index_groups=groups)  9.35 us
    ppermute x1, starting transfers between devices, on_device(): other = lax.ppermute(own, 'site', swap)  8 us
    ppermute x1, starting transfers between devices, on_device(): taken = lax.ppermute(given, 'site', swap)  6.2 us
    unnamed x22, local copies, waits for them, and re-layouts  5.95 us
    all_to_all x1, waiting for transfers between devices, exchange(): return lax.all_to_all(pieces, axis, 0, 0, axis_index_groups=groups)  4.1 us
  transfers between devices with their start and end apart: 3, of which 2 were waited for; matrix products, arithmetic and copies ran while one was open for 0% of the time, Pallas kernels for 5%

profile of v6, /device:TPU:1, one launch (start us, length us, event | category | flops | bytes accessed | tf_op | source)
XLA Modules:
  0.0 105.6 jit_solution(946570662099362083)
XLA Ops:
  0.6 0.0 copy-start
  0.6 2.4 %pack.1 = bf16[16,144,256]{2,1,0:T(8,128)(2,1)} custom-call(bf16[2,32,4608]{2,1,0:T(8,128)(2,1)} %vectors_hbm.1, bf16[2,32,4608]{2,1,0:T(8,128)(2,1)} %images_hbm.1), custom_call_target="tpu_custom_call" | custom-call | bytes 2359296 | tf_op jit(solution)/shard_map/pack/pallas_call | solution.py:289
  3.0 9.4 %all-to-all-start = ((bf16[16,144,256]{2,1,0:T(8,128)(2,1)}), bf16[16,144,256]{2,1,0:T(8,128)(2,1)S(1)}, u32[]{:S(2)}, u32[]{:S(2)}) async-start(bf16[16,144,256]{2,1,0:T(8,128)(2,1)} %pack.1), calls=%async_computation | async-start | bytes 2359296 | tf_op jit(solution)/shard_map/all_to_all | solution.py:302
  12.4 0.0 copy-done
  12.4 0.5 turn_matrix.1.turn_ref
  12.9 0.0 copy-start.1
  12.9 1.3 %copy-done.1 = bf16[1024,1024]{1,0:T(8,128)(2,1)} copy-done((bf16[1024,1024]{1,0:T(8,128)(2,1)}, bf16[1024,1024]{1,0:T(8,128)(2,1)S(1)}, u32[]{:S(2)}) %copy-start.1) | copy-done | bytes 2097176
  14.2 0.3 split_ritz.1
  14.5 0.0 copy-start.7
  14.5 1.0 copy-done.7
  15.5 0.0 copy-start.9
  15.5 1.0 copy-done.9
  16.5 1.1 %left_factors.1 = (bf16[2,1024,512]{2,1,0:T(8,128)(2,1)S(1)}, bf16[2,1024,512]{2,1,0:T(8,128)(2,1)S(1)}) custom-call(f32[2,512,512]{2,1,0:T(8,128)S(1)} %copy-done), custom_call_target="tpu_custom_call" | custom-call | bytes 6291456 | tf_op jit(solution)/shard_map/left_factors/pallas_call | solution.py:289
  17.6 0.0 copy-start.3
  17.6 1.3 %copy-done.3 = bf16[2,1024,512]{2,1,0:T(8,128)(2,1)} copy-done((bf16[2,1024,512]{2,1,0:T(8,128)(2,1)}, bf16[2,1024,512]{2,1,0:T(8,128)(2,1)S(1)}, u32[]{:S(2)}) %copy-start.3) | copy-done | bytes 2097176
  19.0 0.0 copy-start.5
  19.0 1.3 %copy-done.5 = bf16[2,1024,512]{2,1,0:T(8,128)(2,1)} copy-done((bf16[2,1024,512]{2,1,0:T(8,128)(2,1)}, bf16[2,1024,512]{2,1,0:T(8,128)(2,1)S(1)}, u32[]{:S(2)}) %copy-start.5) | copy-done | bytes 2097176
  20.3 4.1 %all-to-all-done.got_ref = bf16[16,144,256]{2,1,0:T(8,128)(2,1)S(1)} async-done(((bf16[16,144,256]{2,1,0:T(8,128)(2,1)}), bf16[16,144,256]{2,1,0:T(8,128)(2,1)S(1)}, u32[]{:S(2)}, u32[]{:S(2)}) %all-to-all-start) | async-done | bytes 1179680 | tf_op jit(solution)/shard_map/all_to_all | solution.py:302
  24.4 0.6 share_given.1
  25.0 0.0 copy-start.2
  25.0 6.2 %collective-permute-start = (bf16[16,128,128]{2,1,0:T(8,128)(2,1)S(1)}, bf16[16,128,128]{2,1,0:T(8,128)(2,1)S(1)}, u32[]{:S(2)}, u32[]{:S(2)}) collective-permute-start(bf16[16,128,128]{2,1,0:T(8,128)(2,1)S(1)} %share_given.1), channel_id=1, source_target_pairs={{0,16},{16,0},{32,48},{48,32},{64,80},{80,64},{96,112},{112,96},{1... | collective-permute-start | bytes 1572872 | tf_op jit(solution)/shard_map/ppermute | solution.py:341
  31.2 0.6 share_kept.1.kept_ref
  31.9 0.0 copy-done.2
  31.9 1.4 %rotate.1.turned_ref = bf16[16,144,128]{2,1,0:T(8,128)(2,1)S(1)} custom-call(bf16[16,144,256]{2,1,0:T(8,128)(2,1)S(1)} %all-to-all-done.got_ref, bf16[1024,1024]{1,0:T(8,128)(2,1)S(1)} %copy-done.2), custom_call_target="tpu_custom_call" | custom-call | flops 1000000000 | bytes 3866624 | tf_op jit(solution)/shard_map/rotate/pallas_call | solution.py:289
  33.3 0.0 collective-permute-done.taken_ref
  33.3 0.1 assemble.1
  33.4 0.0 copy-start.8
  33.4 0.0 copy-start.10
  33.5 21.1 %all_to_all.25.back_ref = bf16[16,272,128]{2,1,0:T(8,128)(2,1)S(1)} all-to-all(bf16[16,272,128]{2,1,0:T(8,128)(2,1)S(1)} %assemble.1), channel_id=1, replica_groups={{15,14,13,12,11,10,9,8,7,6,5,4,3,2,1,0},{31,30,29,28,27,26,25,24,23,22,..., dimensions={0} | all-to-all | bytes 2228224 | tf_op jit(solution)/shard_map/all_to_all | solution.py:302
  54.5 0.1 sum_shares.1
  54.6 9.7 %all_to_all.26.pieces_ref = bf16[4,32,512]{2,1,0:T(8,128)(2,1)S(1)} all-to-all(bf16[4,32,512]{2,1,0:T(8,128)(2,1)S(1)} %sum_shares.1), channel_id=1, replica_groups={{256,128,384,0},{288,160,416,32},{320,192,448,64},{352,224,480,96},{112..., dimensions={0} | all-to-all | bytes 262144 | tf_op jit(solution)/shard_map/all_to_all | solution.py:302
  64.3 0.0 copy-start.6
  64.3 0.0 copy-start.4
  64.3 17.4 %all_to_all.27.pieces_ref = bf16[4,32,512]{2,1,0:T(8,128)(2,1)S(1)} all-to-all(bf16[4,32,512]{2,1,0:T(8,128)(2,1)S(1)} %add_shares.1), channel_id=1, replica_groups={{96,64,32,0},{224,192,160,128},{352,320,288,256},{480,448,416,384},{272..., dimensions={0} | all-to-all | bytes 262144 | tf_op jit(solution)/shard_map/all_to_all | solution.py:302
  81.8 0.0 copy-done.8
  81.8 0.0 copy-done.10
  81.8 0.5 project.1
  82.3 11.5 %all_to_all.28.rows_ref = bf16[16,32,512]{2,1,0:T(8,128)(2,1)S(1)} all-to-all(bf16[16,32,512]{2,1,0:T(8,128)(2,1)S(1)} %project.1), channel_id=1, replica_groups={{15,14,13,12,11,10,9,8,7,6,5,4,3,2,1,0},{31,30,29,28,27,26,25,24,23,22,..., dimensions={0} | all-to-all | bytes 1048576 | tf_op jit(solution)/shard_map/all_to_all | solution.py:302
  93.8 8.0 %collective-permute-start.1 = (bf16[16,32,512]{2,1,0:T(8,128)(2,1)S(1)}, bf16[16,32,512]{2,1,0:T(8,128)(2,1)S(1)}, u32[]{:S(2)}, u32[]{:S(2)}) collective-permute-start(bf16[16,32,512]{2,1,0:T(8,128)(2,1)S(1)} %all_to_all.28.rows_ref), channel_id=1, source_target_pairs={{0,16},{16,0},{32,48},{48,32},{64,80},{80,64},{96,112},{112,96},{1... | collective-permute-start | bytes 1572872 | tf_op jit(solution)/shard_map/ppermute | solution.py:360
  101.8 0.0 copy-done.6
  101.8 0.0 copy-done.4
  101.8 1.2 %finish_own.1.first_ref = f32[2,512,512]{2,1,0:T(8,128)S(1)} custom-call(bf16[16,32,512]{2,1,0:T(8,128)(2,1)S(1)} %all_to_all.28.rows_ref, bf16[2,1024,512]{2,1,0:T(8,128)(2,1)S(1)} %copy-done.4, bf16[2,1024,512]{2,1,0:T(8,128)(2,1)S(1)} %copy-done.6), custom_call_target="tpu_custom_call" | custom-call | flops 1000000000 | bytes 6815744 | tf_op jit(solution)/shard_map/finish_own/pallas_call | solution.py:289
  103.1 0.2 collective-permute-done.1.rows_ref
  103.3 2.3 %finish_other.1 = (f32[2,512,512]{2,1,0:T(8,128)}, bf16[2,32,4608]{2,1,0:T(8,128)(2,1)}) custom-call(bf16[16,32,512]{2,1,0:T(8,128)(2,1)S(1)} %collective-permute-done.1.rows_ref, bf16[2,1024,512]{2,1,0:T(8,128)(2,1)S(1)} %copy-done.4, bf16[2,1024,512]{2,1,0:T(8,128)(2,1)S(1)} %copy-done.6, f32[2,512,512]{2,1,0:T(8,128)S(1)} %finish_own.1.first_ref, ...), custom_call_target="tpu_custom_call" | custom-call | flops 1000000000 | bytes 10616832 | tf_op jit(solution)/shard_map/finish_other/pallas_call | solution.py:289
  (1 shorter events, 0.0 us)
Async XLA Ops:
  0.6 11.8 %copy-start = (f32[2,512,512]{2,1,0:T(8,128)S(1)}, f32[2,512,512]{2,1,0:T(8,128)}, u32[]{:S(2)}) copy-start(f32[2,512,512]{2,1,0:T(8,128)} %ritz_ref.2) | copy-start | bytes 6291460
  3.0 21.3 %all-to-all-start = ((bf16[16,144,256]{2,1,0:T(8,128)(2,1)}), bf16[16,144,256]{2,1,0:T(8,128)(2,1)S(1)}, u32[]{:S(2)}, u32[]{:S(2)}) async-start(bf16[16,144,256]{2,1,0:T(8,128)(2,1)} %pack.1), calls=%async_computation | async-start | bytes 2359296 | tf_op jit(solution)/shard_map/all_to_all | solution.py:302
  12.9 1.3 %copy-start.1 = (bf16[1024,1024]{1,0:T(8,128)(2,1)}, bf16[1024,1024]{1,0:T(8,128)(2,1)S(1)}, u32[]{:S(2)}) copy-start(bf16[1024,1024]{1,0:T(8,128)(2,1)S(1)} %turn_matrix.1.turn_ref) | copy-start | bytes 6291460
  14.5 1.0 copy-start.7
  15.5 1.0 copy-start.9
  17.6 1.3 %copy-start.3 = (bf16[2,1024,512]{2,1,0:T(8,128)(2,1)}, bf16[2,1024,512]{2,1,0:T(8,128)(2,1)S(1)}, u32[]{:S(2)}) copy-start(bf16[2,1024,512]{2,1,0:T(8,128)(2,1)S(1)} %get-tuple-element.26.high_ref) | copy-start | bytes 6291460
  19.0 1.3 %copy-start.5 = (bf16[2,1024,512]{2,1,0:T(8,128)(2,1)}, bf16[2,1024,512]{2,1,0:T(8,128)(2,1)S(1)}, u32[]{:S(2)}) copy-start(bf16[2,1024,512]{2,1,0:T(8,128)(2,1)S(1)} %get-tuple-element.27.low_ref) | copy-start | bytes 6291460
  25.0 6.9 %copy-start.2 = (bf16[1024,1024]{1,0:T(8,128)(2,1)S(1)}, bf16[1024,1024]{1,0:T(8,128)(2,1)}, u32[]{:S(2)}) copy-start(bf16[1024,1024]{1,0:T(8,128)(2,1)} %copy-done.1) | copy-start | bytes 6291460
  25.0 8.3 %collective-permute-start = (bf16[16,128,128]{2,1,0:T(8,128)(2,1)S(1)}, bf16[16,128,128]{2,1,0:T(8,128)(2,1)S(1)}, u32[]{:S(2)}, u32[]{:S(2)}) collective-permute-start(bf16[16,128,128]{2,1,0:T(8,128)(2,1)S(1)} %share_given.1), channel_id=1, source_target_pairs={{0,16},{16,0},{32,48},{48,32},{64,80},{80,64},{96,112},{112,96},{1... | collective-permute-start | bytes 1572872 | tf_op jit(solution)/shard_map/ppermute | solution.py:341
  33.4 48.3 %copy-start.8 = (bf16[2,512,512]{2,1,0:T(8,128)(2,1)S(1)}, bf16[2,512,512]{2,1,0:T(8,128)(2,1)}, u32[]{:S(2)}) copy-start(bf16[2,512,512]{2,1,0:T(8,128)(2,1)} %copy-done.7) | copy-start | bytes 3145732
  33.4 48.3 %copy-start.10 = (bf16[2,512,512]{2,1,0:T(8,128)(2,1)S(1)}, bf16[2,512,512]{2,1,0:T(8,128)(2,1)}, u32[]{:S(2)}) copy-start(bf16[2,512,512]{2,1,0:T(8,128)(2,1)} %copy-done.9) | copy-start | bytes 3145732
  64.3 37.5 %copy-start.6 = (bf16[2,1024,512]{2,1,0:T(8,128)(2,1)S(1)}, bf16[2,1024,512]{2,1,0:T(8,128)(2,1)}, u32[]{:S(2)}) copy-start(bf16[2,1024,512]{2,1,0:T(8,128)(2,1)} %copy-done.5) | copy-start | bytes 6291460
  64.3 37.5 %copy-start.4 = (bf16[2,1024,512]{2,1,0:T(8,128)(2,1)S(1)}, bf16[2,1024,512]{2,1,0:T(8,128)(2,1)}, u32[]{:S(2)}) copy-start(bf16[2,1024,512]{2,1,0:T(8,128)(2,1)} %copy-done.3) | copy-start | bytes 6291460
  93.8 9.5 %collective-permute-start.1 = (bf16[16,32,512]{2,1,0:T(8,128)(2,1)S(1)}, bf16[16,32,512]{2,1,0:T(8,128)(2,1)S(1)}, u32[]{:S(2)}, u32[]{:S(2)}) collective-permute-start(bf16[16,32,512]{2,1,0:T(8,128)(2,1)S(1)} %all_to_all.28.rows_ref), channel_id=1, source_target_pairs={{0,16},{16,0},{32,48},{48,32},{64,80},{80,64},{96,112},{112,96},{1... | collective-permute-start | bytes 1572872 | tf_op jit(solution)/shard_map/ppermute | solution.py:360

commit v7 on v6

--- a/solution.py
+++ b/solution.py
@@ -170,7 +170,8 @@
             out_ref[place, TAIL_ROW:PIECE_ROWS, :] = sent[owner].astype(BF16)
 
 
-def share_kernel(other, got_ref, out_ref, left, right):
+def share_kernel(other, *refs):
+    got_ref, out_ref, right, left = refs if other else (refs[0], refs[2], refs[1], refs[3])
     core = lax.rem(lax.axis_index("site"), 2)
     half = 1 - core if other else core
     group = lane_group((PEERS, HALF, LANES))
@@ -186,8 +187,8 @@
     ends = jnp.where(half == 0, side(packed, 0, (0, 1), (1, 1)), side(packed, 1, (0, 1), (1, 1)))
     left[:, 2 * MAIN : DEPTH] = ends.reshape(HALF_MODES, LANES).astype(BF16)
 
-    packed = tails_of(got_ref, 1, REVERSED)
-    for part in range(2):
+    packed = tails_of(got_ref, 1, REVERSED) if other else None
+    for part in range(2 if other else 0):
         sources, signs = ((0, 1), (1, 1)) if part == 0 else ((1, 0), (1, -1))
         for place in range(2):
             values = main_of(got_ref, 1, sources[place])
@@ -336,10 +337,15 @@
     )
     got, (turn_matrix, left, ritz_split) = lax.optimization_barrier((exchange(packed, "mode", [REVERSED]), factors))
 
-    sides = [pltpu.VMEM((HALF_MODES, DEPTH), BF16), pltpu.VMEM((2, MODES, DEPTH), BF16)]
-    given = call(functools.partial(share_kernel, True), "share_given", [(share, BF16)], got, flops=10**9, scratch=sides)
+    side = [pltpu.VMEM((HALF_MODES, DEPTH), BF16)]
+    factor = ((2, MODES, DEPTH), BF16)
+    given, right = call(
+        functools.partial(share_kernel, True), "share_given", [(share, BF16), factor], got, flops=10**9, scratch=side
+    )
     taken = lax.ppermute(given, "site", swap)
-    kept = call(functools.partial(share_kernel, False), "share_kept", [(share, F32)], got, flops=10**9, scratch=sides)
+    kept = call(
+        functools.partial(share_kernel, False), "share_kept", [(share, F32)], got, right, flops=10**9, scratch=side
+    )
     turned = call(
         rotate_kernel,
         "rotate",

time: 106 us -> 106 us (level)
  no operation moved by 1% of the time
where the time goes in v7:
time: 106 us; the launch traced here: 105 us
  blocking collectives  59.7 us (56%)
  starting transfers between devices  23.4 us (22%)
  Pallas kernels  11.2 us (11%)
  local copies, waits for them, and re-layouts  5.92 us (6%)
  waiting for transfers between devices  4.37 us (4%)
    all_to_all x4, blocking collectives, exchange(): return lax.all_to_all(pieces, axis, 0, 0, axis_index_groups=groups)  59.7 us
    pallas_call x13, Pallas kernels, call(): pl.pallas_call(kernel, name=name, out_shape=outs[0] if single else outs,...  11.2 us
    all_to_all x1, starting transfers between devices, exchange(): return lax.all_to_all(pieces, axis, 0, 0, axis_index_groups=groups)  9.35 us
    ppermute x1, starting transfers between devices, on_device(): other = lax.ppermute(own, 'site', swap)  7.98 us
    ppermute x1, starting transfers between devices, on_device(): taken = lax.ppermute(given, 'site', swap)  6.06 us
    unnamed x22, local copies, waits for them, and re-layouts  5.92 us
    all_to_all x1, waiting for transfers between devices, exchange(): return lax.all_to_all(pieces, axis, 0, 0, axis_index_groups=groups)  4.13 us
  transfers between devices with their start and end apart: 3, of which 2 were waited for; matrix products, arithmetic and copies ran while one was open for 0% of the time, Pallas kernels for 5%

profile of v7, /device:TPU:1, one launch (start us, length us, event | category | flops | bytes accessed | tf_op | source)
XLA Modules:
  0.0 105.5 jit_solution(12224993671436006220)
XLA Ops:
  0.6 0.0 copy-start
  0.6 2.4 %pack.1 = bf16[16,144,256]{2,1,0:T(8,128)(2,1)} custom-call(bf16[2,32,4608]{2,1,0:T(8,128)(2,1)} %vectors_hbm.1, bf16[2,32,4608]{2,1,0:T(8,128)(2,1)} %images_hbm.1), custom_call_target="tpu_custom_call" | custom-call | bytes 2359296 | tf_op jit(solution)/shard_map/pack/pallas_call | solution.py:290
  3.0 9.4 %all-to-all-start = ((bf16[16,144,256]{2,1,0:T(8,128)(2,1)}), bf16[16,144,256]{2,1,0:T(8,128)(2,1)S(1)}, u32[]{:S(2)}, u32[]{:S(2)}) async-start(bf16[16,144,256]{2,1,0:T(8,128)(2,1)} %pack.1), calls=%async_computation | async-start | bytes 2359296 | tf_op jit(solution)/shard_map/all_to_all | solution.py:303
  12.4 0.0 copy-done
  12.4 0.5 turn_matrix.1.turn_ref
  12.9 0.0 copy-start.1
  12.9 1.3 %copy-done.1 = bf16[1024,1024]{1,0:T(8,128)(2,1)} copy-done((bf16[1024,1024]{1,0:T(8,128)(2,1)}, bf16[1024,1024]{1,0:T(8,128)(2,1)S(1)}, u32[]{:S(2)}) %copy-start.1) | copy-done | bytes 2097176
  14.2 0.3 split_ritz.1
  14.5 0.0 copy-start.7
  14.5 1.0 copy-done.7
  15.5 0.0 copy-start.9
  15.5 1.0 copy-done.9
  16.4 1.1 %left_factors.1 = (bf16[2,1024,512]{2,1,0:T(8,128)(2,1)S(1)}, bf16[2,1024,512]{2,1,0:T(8,128)(2,1)S(1)}) custom-call(f32[2,512,512]{2,1,0:T(8,128)S(1)} %copy-done), custom_call_target="tpu_custom_call" | custom-call | bytes 6291456 | tf_op jit(solution)/shard_map/left_factors/pallas_call | solution.py:290
  17.6 0.0 copy-start.3
  17.6 1.3 %copy-done.3 = bf16[2,1024,512]{2,1,0:T(8,128)(2,1)} copy-done((bf16[2,1024,512]{2,1,0:T(8,128)(2,1)}, bf16[2,1024,512]{2,1,0:T(8,128)(2,1)S(1)}, u32[]{:S(2)}) %copy-start.3) | copy-done | bytes 2097176
  18.9 0.0 copy-start.5
  18.9 1.3 %copy-done.5 = bf16[2,1024,512]{2,1,0:T(8,128)(2,1)} copy-done((bf16[2,1024,512]{2,1,0:T(8,128)(2,1)}, bf16[2,1024,512]{2,1,0:T(8,128)(2,1)S(1)}, u32[]{:S(2)}) %copy-start.5) | copy-done | bytes 2097176
  20.2 0.0 copy-start.2
  20.2 4.1 %all-to-all-done.refs_0_.got_ref = bf16[16,144,256]{2,1,0:T(8,128)(2,1)S(1)} async-done(((bf16[16,144,256]{2,1,0:T(8,128)(2,1)}), bf16[16,144,256]{2,1,0:T(8,128)(2,1)S(1)}, u32[]{:S(2)}, u32[]{:S(2)}) %all-to-all-start) | async-done | bytes 1179680 | tf_op jit(solution)/shard_map/all_to_all | solution.py:303
  24.4 0.7 share_given.1
  25.0 6.1 %collective-permute-start = (bf16[16,128,128]{2,1,0:T(8,128)(2,1)S(1)}, bf16[16,128,128]{2,1,0:T(8,128)(2,1)S(1)}, u32[]{:S(2)}, u32[]{:S(2)}) collective-permute-start(bf16[16,128,128]{2,1,0:T(8,128)(2,1)S(1)} %get-tuple-element.26), channel_id=1, source_target_pairs={{0,16},{16,0},{32,48},{48,32},{64,80},{80,64},{96,112},{112,96},{1... | collective-permute-start | bytes 1572872 | tf_op jit(solution)/shard_map/ppermute | solution.py:345
  31.1 0.0 copy-done.2
  31.1 1.4 %rotate.1.turned_ref = bf16[16,144,128]{2,1,0:T(8,128)(2,1)S(1)} custom-call(bf16[16,144,256]{2,1,0:T(8,128)(2,1)S(1)} %all-to-all-done.refs_0_.got_ref, bf16[1024,1024]{1,0:T(8,128)(2,1)S(1)} %copy-done.2), custom_call_target="tpu_custom_call" | custom-call | flops 1000000000 | bytes 3866624 | tf_op jit(solution)/shard_map/rotate/pallas_call | solution.py:290
  32.5 0.6 share_kept.1.kept_ref
  33.1 0.0 collective-permute-done.taken_ref
  33.1 0.1 assemble.1
  33.3 0.0 copy-start.8
  33.3 0.0 copy-start.10
  33.3 21.1 %all_to_all.25.back_ref = bf16[16,272,128]{2,1,0:T(8,128)(2,1)S(1)} all-to-all(bf16[16,272,128]{2,1,0:T(8,128)(2,1)S(1)} %assemble.1), channel_id=1, replica_groups={{15,14,13,12,11,10,9,8,7,6,5,4,3,2,1,0},{31,30,29,28,27,26,25,24,23,22,..., dimensions={0} | all-to-all | bytes 2228224 | tf_op jit(solution)/shard_map/all_to_all | solution.py:303
  54.4 0.1 sum_shares.1
  54.5 9.6 %all_to_all.26.pieces_ref = bf16[4,32,512]{2,1,0:T(8,128)(2,1)S(1)} all-to-all(bf16[4,32,512]{2,1,0:T(8,128)(2,1)S(1)} %sum_shares.1), channel_id=1, replica_groups={{256,128,384,0},{288,160,416,32},{320,192,448,64},{352,224,480,96},{112..., dimensions={0} | all-to-all | bytes 262144 | tf_op jit(solution)/shard_map/all_to_all | solution.py:303
  64.1 0.0 copy-start.6
  64.2 0.0 copy-start.4
  64.2 17.4 %all_to_all.27.pieces_ref = bf16[4,32,512]{2,1,0:T(8,128)(2,1)S(1)} all-to-all(bf16[4,32,512]{2,1,0:T(8,128)(2,1)S(1)} %add_shares.1), channel_id=1, replica_groups={{96,64,32,0},{224,192,160,128},{352,320,288,256},{480,448,416,384},{272..., dimensions={0} | all-to-all | bytes 262144 | tf_op jit(solution)/shard_map/all_to_all | solution.py:303
  81.6 0.0 copy-done.8
  81.6 0.0 copy-done.10
  81.6 0.5 project.1
  82.1 11.5 %all_to_all.28.rows_ref = bf16[16,32,512]{2,1,0:T(8,128)(2,1)S(1)} all-to-all(bf16[16,32,512]{2,1,0:T(8,128)(2,1)S(1)} %project.1), channel_id=1, replica_groups={{15,14,13,12,11,10,9,8,7,6,5,4,3,2,1,0},{31,30,29,28,27,26,25,24,23,22,..., dimensions={0} | all-to-all | bytes 1048576 | tf_op jit(solution)/shard_map/all_to_all | solution.py:303
  93.6 8.0 %collective-permute-start.1 = (bf16[16,32,512]{2,1,0:T(8,128)(2,1)S(1)}, bf16[16,32,512]{2,1,0:T(8,128)(2,1)S(1)}, u32[]{:S(2)}, u32[]{:S(2)}) collective-permute-start(bf16[16,32,512]{2,1,0:T(8,128)(2,1)S(1)} %all_to_all.28.rows_ref), channel_id=1, source_target_pairs={{0,16},{16,0},{32,48},{48,32},{64,80},{80,64},{96,112},{112,96},{1... | collective-permute-start | bytes 1572872 | tf_op jit(solution)/shard_map/ppermute | solution.py:366
  101.6 0.0 copy-done.6
  101.6 0.0 copy-done.4
  101.7 1.2 %finish_own.1.first_ref = f32[2,512,512]{2,1,0:T(8,128)S(1)} custom-call(bf16[16,32,512]{2,1,0:T(8,128)(2,1)S(1)} %all_to_all.28.rows_ref, bf16[2,1024,512]{2,1,0:T(8,128)(2,1)S(1)} %copy-done.4, bf16[2,1024,512]{2,1,0:T(8,128)(2,1)S(1)} %copy-done.6), custom_call_target="tpu_custom_call" | custom-call | flops 1000000000 | bytes 6815744 | tf_op jit(solution)/shard_map/finish_own/pallas_call | solution.py:290
  102.9 0.2 collective-permute-done.1.rows_ref
  103.1 2.3 %finish_other.1 = (f32[2,512,512]{2,1,0:T(8,128)}, bf16[2,32,4608]{2,1,0:T(8,128)(2,1)}) custom-call(bf16[16,32,512]{2,1,0:T(8,128)(2,1)S(1)} %collective-permute-done.1.rows_ref, bf16[2,1024,512]{2,1,0:T(8,128)(2,1)S(1)} %copy-done.4, bf16[2,1024,512]{2,1,0:T(8,128)(2,1)S(1)} %copy-done.6, f32[2,512,512]{2,1,0:T(8,128)S(1)} %finish_own.1.first_ref, ...), custom_call_target="tpu_custom_call" | custom-call | flops 1000000000 | bytes 10616832 | tf_op jit(solution)/shard_map/finish_other/pallas_call | solution.py:290
  (1 shorter events, 0.0 us)
Async XLA Ops:
  0.6 11.8 %copy-start = (f32[2,512,512]{2,1,0:T(8,128)S(1)}, f32[2,512,512]{2,1,0:T(8,128)}, u32[]{:S(2)}) copy-start(f32[2,512,512]{2,1,0:T(8,128)} %ritz_ref.2) | copy-start | bytes 6291460
  3.0 21.3 %all-to-all-start = ((bf16[16,144,256]{2,1,0:T(8,128)(2,1)}), bf16[16,144,256]{2,1,0:T(8,128)(2,1)S(1)}, u32[]{:S(2)}, u32[]{:S(2)}) async-start(bf16[16,144,256]{2,1,0:T(8,128)(2,1)} %pack.1), calls=%async_computation | async-start | bytes 2359296 | tf_op jit(solution)/shard_map/all_to_all | solution.py:303
  12.9 1.3 %copy-start.1 = (bf16[1024,1024]{1,0:T(8,128)(2,1)}, bf16[1024,1024]{1,0:T(8,128)(2,1)S(1)}, u32[]{:S(2)}) copy-start(bf16[1024,1024]{1,0:T(8,128)(2,1)S(1)} %turn_matrix.1.turn_ref) | copy-start | bytes 6291460
  14.5 1.0 copy-start.7
  15.5 1.0 copy-start.9
  17.6 1.3 %copy-start.3 = (bf16[2,1024,512]{2,1,0:T(8,128)(2,1)}, bf16[2,1024,512]{2,1,0:T(8,128)(2,1)S(1)}, u32[]{:S(2)}) copy-start(bf16[2,1024,512]{2,1,0:T(8,128)(2,1)S(1)} %get-tuple-element.30.high_ref) | copy-start | bytes 6291460
  18.9 1.3 %copy-start.5 = (bf16[2,1024,512]{2,1,0:T(8,128)(2,1)}, bf16[2,1024,512]{2,1,0:T(8,128)(2,1)S(1)}, u32[]{:S(2)}) copy-start(bf16[2,1024,512]{2,1,0:T(8,128)(2,1)S(1)} %get-tuple-element.31.low_ref) | copy-start | bytes 6291460
  20.2 10.9 %copy-start.2 = (bf16[1024,1024]{1,0:T(8,128)(2,1)S(1)}, bf16[1024,1024]{1,0:T(8,128)(2,1)}, u32[]{:S(2)}) copy-start(bf16[1024,1024]{1,0:T(8,128)(2,1)} %copy-done.1) | copy-start | bytes 6291460
  25.0 8.1 %collective-permute-start = (bf16[16,128,128]{2,1,0:T(8,128)(2,1)S(1)}, bf16[16,128,128]{2,1,0:T(8,128)(2,1)S(1)}, u32[]{:S(2)}, u32[]{:S(2)}) collective-permute-start(bf16[16,128,128]{2,1,0:T(8,128)(2,1)S(1)} %get-tuple-element.26), channel_id=1, source_target_pairs={{0,16},{16,0},{32,48},{48,32},{64,80},{80,64},{96,112},{112,96},{1... | collective-permute-start | bytes 1572872 | tf_op jit(solution)/shard_map/ppermute | solution.py:345
  33.3 48.4 %copy-start.8 = (bf16[2,512,512]{2,1,0:T(8,128)(2,1)S(1)}, bf16[2,512,512]{2,1,0:T(8,128)(2,1)}, u32[]{:S(2)}) copy-start(bf16[2,512,512]{2,1,0:T(8,128)(2,1)} %copy-done.7) | copy-start | bytes 3145732
  33.3 48.3 %copy-start.10 = (bf16[2,512,512]{2,1,0:T(8,128)(2,1)S(1)}, bf16[2,512,512]{2,1,0:T(8,128)(2,1)}, u32[]{:S(2)}) copy-start(bf16[2,512,512]{2,1,0:T(8,128)(2,1)} %copy-done.9) | copy-start | bytes 3145732
  64.1 37.5 %copy-start.6 = (bf16[2,1024,512]{2,1,0:T(8,128)(2,1)S(1)}, bf16[2,1024,512]{2,1,0:T(8,128)(2,1)}, u32[]{:S(2)}) copy-start(bf16[2,1024,512]{2,1,0:T(8,128)(2,1)} %copy-done.5) | copy-start | bytes 6291460
  64.2 37.5 %copy-start.4 = (bf16[2,1024,512]{2,1,0:T(8,128)(2,1)S(1)}, bf16[2,1024,512]{2,1,0:T(8,128)(2,1)}, u32[]{:S(2)}) copy-start(bf16[2,1024,512]{2,1,0:T(8,128)(2,1)} %copy-done.3) | copy-start | bytes 6291460
  93.6 9.5 %collective-permute-start.1 = (bf16[16,32,512]{2,1,0:T(8,128)(2,1)S(1)}, bf16[16,32,512]{2,1,0:T(8,128)(2,1)S(1)}, u32[]{:S(2)}, u32[]{:S(2)}) collective-permute-start(bf16[16,32,512]{2,1,0:T(8,128)(2,1)S(1)} %all_to_all.28.rows_ref), channel_id=1, source_target_pairs={{0,16},{16,0},{32,48},{48,32},{64,80},{80,64},{96,112},{112,96},{1... | collective-permute-start | bytes 1572872 | tf_op jit(solution)/shard_map/ppermute | solution.py:366

commit v8 on v7

--- a/solution.py
+++ b/solution.py
@@ -264,7 +264,9 @@
 
 def finish_other_kernel(rows_ref, high_ref, low_ref, first_ref, back_ref, out_hbm, rotated_hbm, total, rotated, sent):
     core = lax.rem(lax.axis_index("site"), 2)
-    copies = []
+    unpack_kernel(back_ref, rotated)
+    copies = [pltpu.make_async_copy(rotated, rotated_hbm, sent.at[4])]
+    copies[0].start()
     for part in range(2):
         for half in range(2):
             rows = pl.ds(half * HALF_MODES, HALF_MODES)
@@ -273,11 +275,8 @@
             copy = pltpu.make_async_copy(total.at[part, rows, :], out_hbm.at[part, rows, :], sent.at[part * 2 + half])
             copy.start()
             copies.append(copy)
-    unpack_kernel(back_ref, rotated)
-    copy = pltpu.make_async_copy(rotated, rotated_hbm, sent.at[4])
-    copy.start()
-    for done in copies + [copy]:
-        done.wait()
+    for copy in copies:
+        copy.wait()
 
 
 def call(kernel, name, outs, *args, flops=0, scratch=(), in_place=False, out_place=False, vmem=16):

time: 106 us -> 106 us (level)
  no operation moved by 1% of the time
where the time goes in v8:
time: 106 us; the launch traced here: 105 us
  blocking collectives  59.7 us (56%)
  starting transfers between devices  23.4 us (22%)
  Pallas kernels  11.1 us (10%)
  local copies, waits for them, and re-layouts  5.92 us (6%)
  waiting for transfers between devices  4.37 us (4%)
    all_to_all x4, blocking collectives, exchange(): return lax.all_to_all(pieces, axis, 0, 0, axis_index_groups=groups)  59.7 us
    pallas_call x13, Pallas kernels, call(): pl.pallas_call(kernel, name=name, out_shape=outs[0] if single else outs,...  11.1 us
    all_to_all x1, starting transfers between devices, exchange(): return lax.all_to_all(pieces, axis, 0, 0, axis_index_groups=groups)  9.35 us
    ppermute x1, starting transfers between devices, on_device(): other = lax.ppermute(own, 'site', swap)  7.98 us
    ppermute x1, starting transfers between devices, on_device(): taken = lax.ppermute(given, 'site', swap)  6.06 us
    unnamed x22, local copies, waits for them, and re-layouts  5.92 us
    all_to_all x1, waiting for transfers between devices, exchange(): return lax.all_to_all(pieces, axis, 0, 0, axis_index_groups=groups)  4.13 us
  transfers between devices with their start and end apart: 3, of which 2 were waited for; matrix products, arithmetic and copies ran while one was open for 0% of the time, Pallas kernels for 5%

profile of v8, /device:TPU:1, one launch (start us, length us, event | category | flops | bytes accessed | tf_op | source)
XLA Modules:
  0.0 105.4 jit_solution(9169059054875344882)
XLA Ops:
  0.6 0.0 copy-start
  0.6 2.4 %pack.1 = bf16[16,144,256]{2,1,0:T(8,128)(2,1)} custom-call(bf16[2,32,4608]{2,1,0:T(8,128)(2,1)} %vectors_hbm.1, bf16[2,32,4608]{2,1,0:T(8,128)(2,1)} %images_hbm.1), custom_call_target="tpu_custom_call" | custom-call | bytes 2359296 | tf_op jit(solution)/shard_map/pack/pallas_call | solution.py:289
  3.0 9.4 %all-to-all-start = ((bf16[16,144,256]{2,1,0:T(8,128)(2,1)}), bf16[16,144,256]{2,1,0:T(8,128)(2,1)S(1)}, u32[]{:S(2)}, u32[]{:S(2)}) async-start(bf16[16,144,256]{2,1,0:T(8,128)(2,1)} %pack.1), calls=%async_computation | async-start | bytes 2359296 | tf_op jit(solution)/shard_map/all_to_all | solution.py:302
  12.4 0.0 copy-done
  12.4 0.5 turn_matrix.1.turn_ref
  12.9 0.0 copy-start.1
  12.9 1.3 %copy-done.1 = bf16[1024,1024]{1,0:T(8,128)(2,1)} copy-done((bf16[1024,1024]{1,0:T(8,128)(2,1)}, bf16[1024,1024]{1,0:T(8,128)(2,1)S(1)}, u32[]{:S(2)}) %copy-start.1) | copy-done | bytes 2097176
  14.2 0.3 split_ritz.1
  14.5 0.0 copy-start.7
  14.5 1.0 copy-done.7
  15.5 0.0 copy-start.9
  15.5 1.0 copy-done.9
  16.4 1.1 %left_factors.1 = (bf16[2,1024,512]{2,1,0:T(8,128)(2,1)S(1)}, bf16[2,1024,512]{2,1,0:T(8,128)(2,1)S(1)}) custom-call(f32[2,512,512]{2,1,0:T(8,128)S(1)} %copy-done), custom_call_target="tpu_custom_call" | custom-call | bytes 6291456 | tf_op jit(solution)/shard_map/left_factors/pallas_call | solution.py:289
  17.6 0.0 copy-start.3
  17.6 1.3 %copy-done.3 = bf16[2,1024,512]{2,1,0:T(8,128)(2,1)} copy-done((bf16[2,1024,512]{2,1,0:T(8,128)(2,1)}, bf16[2,1024,512]{2,1,0:T(8,128)(2,1)S(1)}, u32[]{:S(2)}) %copy-start.3) | copy-done | bytes 2097176
  18.9 0.0 copy-start.5
  18.9 1.3 %copy-done.5 = bf16[2,1024,512]{2,1,0:T(8,128)(2,1)} copy-done((bf16[2,1024,512]{2,1,0:T(8,128)(2,1)}, bf16[2,1024,512]{2,1,0:T(8,128)(2,1)S(1)}, u32[]{:S(2)}) %copy-start.5) | copy-done | bytes 2097176
  20.2 0.0 copy-start.2
  20.2 4.1 %all-to-all-done.refs_0_.got_ref = bf16[16,144,256]{2,1,0:T(8,128)(2,1)S(1)} async-done(((bf16[16,144,256]{2,1,0:T(8,128)(2,1)}), bf16[16,144,256]{2,1,0:T(8,128)(2,1)S(1)}, u32[]{:S(2)}, u32[]{:S(2)}) %all-to-all-start) | async-done | bytes 1179680 | tf_op jit(solution)/shard_map/all_to_all | solution.py:302
  24.4 0.7 share_given.1
  25.0 6.1 %collective-permute-start = (bf16[16,128,128]{2,1,0:T(8,128)(2,1)S(1)}, bf16[16,128,128]{2,1,0:T(8,128)(2,1)S(1)}, u32[]{:S(2)}, u32[]{:S(2)}) collective-permute-start(bf16[16,128,128]{2,1,0:T(8,128)(2,1)S(1)} %get-tuple-element.26), channel_id=1, source_target_pairs={{0,16},{16,0},{32,48},{48,32},{64,80},{80,64},{96,112},{112,96},{1... | collective-permute-start | bytes 1572872 | tf_op jit(solution)/shard_map/ppermute | solution.py:344
  31.1 0.0 copy-done.2
  31.1 1.4 %rotate.1.turned_ref = bf16[16,144,128]{2,1,0:T(8,128)(2,1)S(1)} custom-call(bf16[16,144,256]{2,1,0:T(8,128)(2,1)S(1)} %all-to-all-done.refs_0_.got_ref, bf16[1024,1024]{1,0:T(8,128)(2,1)S(1)} %copy-done.2), custom_call_target="tpu_custom_call" | custom-call | flops 1000000000 | bytes 3866624 | tf_op jit(solution)/shard_map/rotate/pallas_call | solution.py:289
  32.5 0.6 share_kept.1.kept_ref
  33.1 0.0 collective-permute-done.taken_ref
  33.1 0.1 assemble.1
  33.3 0.0 copy-start.8
  33.3 0.0 copy-start.10
  33.3 21.1 %all_to_all.25.back_ref = bf16[16,272,128]{2,1,0:T(8,128)(2,1)S(1)} all-to-all(bf16[16,272,128]{2,1,0:T(8,128)(2,1)S(1)} %assemble.1), channel_id=1, replica_groups={{15,14,13,12,11,10,9,8,7,6,5,4,3,2,1,0},{31,30,29,28,27,26,25,24,23,22,..., dimensions={0} | all-to-all | bytes 2228224 | tf_op jit(solution)/shard_map/all_to_all | solution.py:302
  54.4 0.1 sum_shares.1
  54.5 9.6 %all_to_all.26.pieces_ref = bf16[4,32,512]{2,1,0:T(8,128)(2,1)S(1)} all-to-all(bf16[4,32,512]{2,1,0:T(8,128)(2,1)S(1)} %sum_shares.1), channel_id=1, replica_groups={{256,128,384,0},{288,160,416,32},{320,192,448,64},{352,224,480,96},{112..., dimensions={0} | all-to-all | bytes 262144 | tf_op jit(solution)/shard_map/all_to_all | solution.py:302
  64.1 0.0 copy-start.6
  64.2 0.0 copy-start.4
  64.2 17.4 %all_to_all.27.pieces_ref = bf16[4,32,512]{2,1,0:T(8,128)(2,1)S(1)} all-to-all(bf16[4,32,512]{2,1,0:T(8,128)(2,1)S(1)} %add_shares.1), channel_id=1, replica_groups={{96,64,32,0},{224,192,160,128},{352,320,288,256},{480,448,416,384},{272..., dimensions={0} | all-to-all | bytes 262144 | tf_op jit(solution)/shard_map/all_to_all | solution.py:302
  81.6 0.0 copy-done.8
  81.6 0.0 copy-done.10
  81.6 0.5 project.1
  82.1 11.5 %all_to_all.28.rows_ref = bf16[16,32,512]{2,1,0:T(8,128)(2,1)S(1)} all-to-all(bf16[16,32,512]{2,1,0:T(8,128)(2,1)S(1)} %project.1), channel_id=1, replica_groups={{15,14,13,12,11,10,9,8,7,6,5,4,3,2,1,0},{31,30,29,28,27,26,25,24,23,22,..., dimensions={0} | all-to-all | bytes 1048576 | tf_op jit(solution)/shard_map/all_to_all | solution.py:302
  93.6 8.0 %collective-permute-start.1 = (bf16[16,32,512]{2,1,0:T(8,128)(2,1)S(1)}, bf16[16,32,512]{2,1,0:T(8,128)(2,1)S(1)}, u32[]{:S(2)}, u32[]{:S(2)}) collective-permute-start(bf16[16,32,512]{2,1,0:T(8,128)(2,1)S(1)} %all_to_all.28.rows_ref), channel_id=1, source_target_pairs={{0,16},{16,0},{32,48},{48,32},{64,80},{80,64},{96,112},{112,96},{1... | collective-permute-start | bytes 1572872 | tf_op jit(solution)/shard_map/ppermute | solution.py:365
  101.6 0.0 copy-done.6
  101.6 0.0 copy-done.4
  101.7 1.2 %finish_own.1.first_ref = f32[2,512,512]{2,1,0:T(8,128)S(1)} custom-call(bf16[16,32,512]{2,1,0:T(8,128)(2,1)S(1)} %all_to_all.28.rows_ref, bf16[2,1024,512]{2,1,0:T(8,128)(2,1)S(1)} %copy-done.4, bf16[2,1024,512]{2,1,0:T(8,128)(2,1)S(1)} %copy-done.6), custom_call_target="tpu_custom_call" | custom-call | flops 1000000000 | bytes 6815744 | tf_op jit(solution)/shard_map/finish_own/pallas_call | solution.py:289
  102.9 0.2 collective-permute-done.1.rows_ref
  103.1 2.2 %finish_other.1 = (f32[2,512,512]{2,1,0:T(8,128)}, bf16[2,32,4608]{2,1,0:T(8,128)(2,1)}) custom-call(bf16[16,32,512]{2,1,0:T(8,128)(2,1)S(1)} %collective-permute-done.1.rows_ref, bf16[2,1024,512]{2,1,0:T(8,128)(2,1)S(1)} %copy-done.4, bf16[2,1024,512]{2,1,0:T(8,128)(2,1)S(1)} %copy-done.6, f32[2,512,512]{2,1,0:T(8,128)S(1)} %finish_own.1.first_ref, ...), custom_call_target="tpu_custom_call" | custom-call | flops 1000000000 | bytes 10616832 | tf_op jit(solution)/shard_map/finish_other/pallas_call | solution.py:289
  (1 shorter events, 0.0 us)
Async XLA Ops:
  0.6 11.8 %copy-start = (f32[2,512,512]{2,1,0:T(8,128)S(1)}, f32[2,512,512]{2,1,0:T(8,128)}, u32[]{:S(2)}) copy-start(f32[2,512,512]{2,1,0:T(8,128)} %ritz_ref.2) | copy-start | bytes 6291460
  3.0 21.3 %all-to-all-start = ((bf16[16,144,256]{2,1,0:T(8,128)(2,1)}), bf16[16,144,256]{2,1,0:T(8,128)(2,1)S(1)}, u32[]{:S(2)}, u32[]{:S(2)}) async-start(bf16[16,144,256]{2,1,0:T(8,128)(2,1)} %pack.1), calls=%async_computation | async-start | bytes 2359296 | tf_op jit(solution)/shard_map/all_to_all | solution.py:302
  12.9 1.3 %copy-start.1 = (bf16[1024,1024]{1,0:T(8,128)(2,1)}, bf16[1024,1024]{1,0:T(8,128)(2,1)S(1)}, u32[]{:S(2)}) copy-start(bf16[1024,1024]{1,0:T(8,128)(2,1)S(1)} %turn_matrix.1.turn_ref) | copy-start | bytes 6291460
  14.5 1.0 copy-start.7
  15.5 1.0 copy-start.9
  17.6 1.3 %copy-start.3 = (bf16[2,1024,512]{2,1,0:T(8,128)(2,1)}, bf16[2,1024,512]{2,1,0:T(8,128)(2,1)S(1)}, u32[]{:S(2)}) copy-start(bf16[2,1024,512]{2,1,0:T(8,128)(2,1)S(1)} %get-tuple-element.30.high_ref) | copy-start | bytes 6291460
  18.9 1.3 %copy-start.5 = (bf16[2,1024,512]{2,1,0:T(8,128)(2,1)}, bf16[2,1024,512]{2,1,0:T(8,128)(2,1)S(1)}, u32[]{:S(2)}) copy-start(bf16[2,1024,512]{2,1,0:T(8,128)(2,1)S(1)} %get-tuple-element.31.low_ref) | copy-start | bytes 6291460
  20.2 10.9 %copy-start.2 = (bf16[1024,1024]{1,0:T(8,128)(2,1)S(1)}, bf16[1024,1024]{1,0:T(8,128)(2,1)}, u32[]{:S(2)}) copy-start(bf16[1024,1024]{1,0:T(8,128)(2,1)} %copy-done.1) | copy-start | bytes 6291460
  25.0 8.1 %collective-permute-start = (bf16[16,128,128]{2,1,0:T(8,128)(2,1)S(1)}, bf16[16,128,128]{2,1,0:T(8,128)(2,1)S(1)}, u32[]{:S(2)}, u32[]{:S(2)}) collective-permute-start(bf16[16,128,128]{2,1,0:T(8,128)(2,1)S(1)} %get-tuple-element.26), channel_id=1, source_target_pairs={{0,16},{16,0},{32,48},{48,32},{64,80},{80,64},{96,112},{112,96},{1... | collective-permute-start | bytes 1572872 | tf_op jit(solution)/shard_map/ppermute | solution.py:344
  33.3 48.4 %copy-start.8 = (bf16[2,512,512]{2,1,0:T(8,128)(2,1)S(1)}, bf16[2,512,512]{2,1,0:T(8,128)(2,1)}, u32[]{:S(2)}) copy-start(bf16[2,512,512]{2,1,0:T(8,128)(2,1)} %copy-done.7) | copy-start | bytes 3145732
  33.3 48.3 %copy-start.10 = (bf16[2,512,512]{2,1,0:T(8,128)(2,1)S(1)}, bf16[2,512,512]{2,1,0:T(8,128)(2,1)}, u32[]{:S(2)}) copy-start(bf16[2,512,512]{2,1,0:T(8,128)(2,1)} %copy-done.9) | copy-start | bytes 3145732
  64.1 37.5 %copy-start.6 = (bf16[2,1024,512]{2,1,0:T(8,128)(2,1)S(1)}, bf16[2,1024,512]{2,1,0:T(8,128)(2,1)}, u32[]{:S(2)}) copy-start(bf16[2,1024,512]{2,1,0:T(8,128)(2,1)} %copy-done.5) | copy-start | bytes 6291460
  64.2 37.5 %copy-start.4 = (bf16[2,1024,512]{2,1,0:T(8,128)(2,1)S(1)}, bf16[2,1024,512]{2,1,0:T(8,128)(2,1)}, u32[]{:S(2)}) copy-start(bf16[2,1024,512]{2,1,0:T(8,128)(2,1)} %copy-done.3) | copy-start | bytes 6291460
  93.6 9.5 %collective-permute-start.1 = (bf16[16,32,512]{2,1,0:T(8,128)(2,1)S(1)}, bf16[16,32,512]{2,1,0:T(8,128)(2,1)S(1)}, u32[]{:S(2)}, u32[]{:S(2)}) collective-permute-start(bf16[16,32,512]{2,1,0:T(8,128)(2,1)S(1)} %all_to_all.28.rows_ref), channel_id=1, source_target_pairs={{0,16},{16,0},{32,48},{48,32},{64,80},{80,64},{96,112},{112,96},{1... | collective-permute-start | bytes 1572872 | tf_op jit(solution)/shard_map/ppermute | solution.py:365
